TPU v7x, 512 devices: a whole 4x4x16 slice. The times are simulated.
512 devices in a mesh: gx: 64 (over z, y), yz: 8 (over x, core).
Axes of the slice: x: 4, y: 4, z: 16, core: 2. Of those that a mesh axis runs over, the one named last changes fastest.
Arguments:
- velocity: float32 [3, 4096, 16384], P(None, 'gx', 'yz'), may hold values from -45 to 45
- blocks: float32 [64, 62, 62], P('gx'), may hold values from -10 to 10, as said below
Outputs:
- derivative: float32 [3, 4096, 16384], P(None, 'gx', 'yz')
- mean_square: float32 [], replicated
Inputs may be any that keep to these rules, and one draw needn't show every extreme that they name: `blocks`: every row of the reduced system is strictly diagonally dominant.
All inputs are finite; a program needn't handle non-finite values.
Results may differ from a plain program's by a relative error of at most 0.0003.
Values sent between devices are 32-bit elements; how exact they have to be, the bound alone decides.
No kernel may reach another device: no remote copies, remote signals or barrier semaphores. Data moves between devices by JAX's collectives and lax.ppermute only.
A program may use at most 64 MiB of HBM per device.

v0:
```python
import jax
import jax.numpy as jnp
from jax import lax
from jax.sharding import PartitionSpec as P

COUPLING = 1.0 / 3.0
NEAR_WEIGHT = 7.0 / 9.0
FAR_WEIGHT = 1.0 / 36.0


def passed_along(value, axis, steps):
    count = lax.axis_size(axis)
    pairs = [(source, (source + steps) % count) for source in range(count)]
    return lax.ppermute(value, axis, pairs)


def padded_2(block, sides, width):
    for axis, dim in sides:
        count = lax.axis_size(axis)
        forward = [(i, i + 1) for i in range(count - 1)]
        forward.append((count - 1, 0))
        backward = [(target, source) for source, target in forward]
        low = lax.ppermute(
            lax.slice_in_dim(block, block.shape[dim] - width, None, axis=dim), axis, forward
        )
        high = lax.ppermute(lax.slice_in_dim(block, 0, width, axis=dim), axis, backward)
        block = jnp.concatenate([low, block, high], axis=dim)
    return block


def reduce_level(state, below, above):
    lower_coef, diag_coef, upper_coef, right_rows = state
    below_lower, below_diag, below_upper, below_right = below
    above_lower, above_diag, above_upper, above_right = above
    ratio_low = lower_coef / below_diag
    ratio_high = upper_coef / above_diag
    new_lower = -ratio_low * below_lower
    new_upper = -ratio_high * above_upper
    new_diag = diag_coef - ratio_low * below_upper - ratio_high * above_lower
    new_right = right_rows - ratio_low * below_right - ratio_high * above_right
    return (new_lower, new_diag, new_upper, new_right)


def neighbours(state, distance):
    before = passed_along((state[0], state[1], state[2], state[3]), "gx", distance)
    after = passed_along((state[0], state[1], state[2], state[3]), "gx", -distance)
    return (before, after)


def doubling_solve(state):
    count = lax.axis_size("gx")
    before, after = neighbours(state, 1)
    below = tuple(
        (jnp.concatenate([theirs[1:2], mine[0:1]], 0) for theirs, mine in zip(before, state))
    )
    above = tuple(
        (jnp.concatenate([mine[1:2], theirs[0:1]], 0) for theirs, mine in zip(after, state))
    )
    state = reduce_level(state, below, above)
    for bit_pos in range(count.bit_length() - 1):
        before, after = neighbours(state, 1 << bit_pos)
        state = reduce_level(state, before, after)
    return state[3] / (state[0] + state[1] + state[2])


def on_device(velocity, blocks):
    cells = velocity.shape[1]
    inner_count = cells - 2
    lines = velocity.shape[2]
    padded = padded_2(velocity, (("gx", 1),), 2)
    right = NEAR_WEIGHT * (padded[:, 3 : cells + 3] - padded[:, 1 : cells + 1]) + FAR_WEIGHT * (
        padded[:, 4 : cells + 4] - padded[:, 0:cells]
    )
    block = blocks[0]
    solved_int = jnp.einsum(
        "ij,cjl->cil", block, right[:, 1 : cells - 1], precision=lax.Precision.HIGHEST
    )
    first_col = COUPLING * block[:, 0]
    last_col = COUPLING * block[:, inner_count - 1]
    lower_coef = jnp.stack(
        [jnp.full((), COUPLING, jnp.float32), -COUPLING * first_col[inner_count - 1]]
    ).reshape(2, 1, 1)
    diag_coef = jnp.stack(
        [1.0 - COUPLING * first_col[0], 1.0 - COUPLING * last_col[inner_count - 1]]
    ).reshape(2, 1, 1)
    upper_coef = jnp.stack([-COUPLING * last_col[0], jnp.full((), COUPLING, jnp.float32)]).reshape(
        2, 1, 1
    )
    right_first = right[:, 0] - COUPLING * solved_int[:, 0]
    right_last = right[:, cells - 1] - COUPLING * solved_int[:, inner_count - 1]
    reduced = jnp.stack([right_first, right_last], 0)
    ends = doubling_solve((lower_coef, diag_coef, upper_coef, reduced))
    first_val = ends[0][:, None, :]
    last_val = ends[1][:, None, :]
    inner = solved_int - first_col[None, :, None] * first_val - last_col[None, :, None] * last_val
    derivative = jnp.concatenate([first_val, inner, last_val], 1)
    total_count = velocity.shape[0] * cells * lines * lax.axis_size("gx") * lax.axis_size("yz")
    energy_sum = lax.psum(jnp.sum(derivative * derivative), ("gx", "yz"))
    return (derivative, energy_sum / total_count)


def solution(mesh):
    placed = (P(None, "gx", "yz"), P("gx", None, None))
    return jax.shard_map(
        on_device, mesh=mesh, in_specs=placed, out_specs=(P(None, "gx", "yz"), P()), check_vma=False
    )
```

profile of v0, /device:TPU:1, one launch (start us, length us, event | category | flops | bytes accessed | tf_op | source)
XLA Modules:
  0.0 399.1 jit_solution(13501497632938549398)
XLA Ops:
  7.4 12.3 %collective-permute-start.11 = (f32[2,1,1]{2,1,0:T(1,128)}, f32[2,1,1]{2,1,0:T(1,128)}, u32[]{:S(2)}, u32[]{:S(2)}) collective-permute-start(f32[2,1,1]{2,1,0:T(1,128)} %copy.21), channel_id=1, source_target_pairs={{0,504},{8,0},{16,8},{24,16},{32,24},{40,32},{48,40},{56,48},{64,5... | collective-permute-start | bytes 32 | tf_op jit(solution)/shard_map/ppermute | solution.py:14
  24.0 6.7 %collective-permute-start.4 = (f32[2,1,1]{0,2,1:T(1,128)S(1)}, f32[2,1,1]{0,2,1:T(1,128)S(1)}, u32[]{:S(2)}, u32[]{:S(2)}) collective-permute-start(f32[2,1,1]{0,2,1:T(1,128)S(1)} %maximum_bitcast_fusion), channel_id=1, source_target_pairs={{0,504},{8,0},{16,8},{24,16},{32,24},{40,32},{48,40},{56,48},{64,5... | collective-permute-start | bytes 32 | tf_op jit(solution)/shard_map/ppermute | solution.py:14
  47.7 4.5 %collective-permute-done.6 = f32[2,1,1]{2,1,0:T(1,128)S(1)} collective-permute-done((f32[2,1,1]{2,1,0:T(1,128)S(1)}, f32[2,1,1]{2,1,0:T(1,128)S(1)}, u32[]{:S(2)}, u32[]{:S(2)}) %collective-permute-start.6) | collective-permute-done | bytes 40 | tf_op jit(solution)/shard_map/ppermute | solution.py:14
  79.9 5.5 %collective-permute-start.12 = (f32[2,1,1]{0,2,1:T(1,128)}, f32[2,1,1]{0,2,1:T(1,128)S(1)}, u32[]{:S(2)}, u32[]{:S(2)}) collective-permute-start(f32[2,1,1]{0,2,1:T(1,128)} %get-tuple-element.31), channel_id=1, source_target_pairs={{0,504},{8,0},{16,8},{24,16},{32,24},{40,32},{48,40},{56,48},{64,5... | collective-permute-start | bytes 32 | tf_op jit(solution)/shard_map/ppermute | solution.py:14
  88.1 6.7 %collective-permute-start.19 = (f32[2,1,1]{0,2,1:T(1,128)S(1)}, f32[2,1,1]{0,2,1:T(1,128)S(1)}, u32[]{:S(2)}, u32[]{:S(2)}) collective-permute-start(f32[2,1,1]{0,2,1:T(1,128)S(1)} %negate_multiply_fusion.10), channel_id=1, source_target_pairs={{0,504},{8,0},{16,8},{24,16},{32,24},{40,32},{48,40},{56,48},{64,5... | collective-permute-start | bytes 32 | tf_op jit(solution)/shard_map/ppermute | solution.py:14
  96.7 4.9 %collective-permute-start.22 = (f32[2,1,1]{0,2,1:T(1,128)S(1)}, f32[2,1,1]{0,2,1:T(1,128)S(1)}, u32[]{:S(2)}, u32[]{:S(2)}) collective-permute-start(f32[2,1,1]{0,2,1:T(1,128)S(1)} %get-tuple-element.25), channel_id=1, source_target_pairs={{0,16},{8,24},{16,32},{24,40},{32,48},{40,56},{48,64},{56,72},{64,... | collective-permute-start | bytes 32 | tf_op jit(solution)/shard_map/ppermute | solution.py:14
  104.6 6.5 %collective-permute-start.20 = (f32[2,1,1]{0,2,1:T(1,128)S(1)}, f32[2,1,1]{0,2,1:T(1,128)S(1)}, u32[]{:S(2)}, u32[]{:S(2)}) collective-permute-start(f32[2,1,1]{0,2,1:T(1,128)S(1)} %get-tuple-element.27), channel_id=1, source_target_pairs={{0,496},{8,504},{16,0},{24,8},{32,16},{40,24},{48,32},{56,40},{64,... | collective-permute-start | bytes 32 | tf_op jit(solution)/shard_map/ppermute | solution.py:14
  113.2 7.0 %collective-permute-start.27 = (f32[2,1,1]{0,2,1:T(1,128)S(1)}, f32[2,1,1]{0,2,1:T(1,128)S(1)}, u32[]{:S(2)}, u32[]{:S(2)}) collective-permute-start(f32[2,1,1]{0,2,1:T(1,128)S(1)} %negate_multiply_fusion.8), channel_id=1, source_target_pairs={{0,496},{8,504},{16,0},{24,8},{32,16},{40,24},{48,32},{56,40},{64,... | collective-permute-start | bytes 32 | tf_op jit(solution)/shard_map/ppermute | solution.py:14
  127.6 4.4 %collective-permute-start.28 = (f32[2,1,1]{0,2,1:T(1,128)S(1)}, f32[2,1,1]{0,2,1:T(1,128)S(1)}, u32[]{:S(2)}, u32[]{:S(2)}) collective-permute-start(f32[2,1,1]{0,2,1:T(1,128)S(1)} %get-tuple-element.23), channel_id=1, source_target_pairs={{0,480},{8,488},{16,496},{24,504},{32,0},{40,8},{48,16},{56,24},{6... | collective-permute-start | bytes 32 | tf_op jit(solution)/shard_map/ppermute | solution.py:14
  134.0 4.6 %collective-permute-start.35 = (f32[2,1,1]{0,2,1:T(1,128)S(1)}, f32[2,1,1]{0,2,1:T(1,128)S(1)}, u32[]{:S(2)}, u32[]{:S(2)}) collective-permute-start(f32[2,1,1]{0,2,1:T(1,128)S(1)} %negate_multiply_fusion.6), channel_id=1, source_target_pairs={{0,480},{8,488},{16,496},{24,504},{32,0},{40,8},{48,16},{56,24},{6... | collective-permute-start | bytes 32 | tf_op jit(solution)/shard_map/ppermute | solution.py:14
  146.8 5.5 %collective-permute-start.36 = (f32[2,1,1]{0,2,1:T(1,128)S(1)}, f32[2,1,1]{0,2,1:T(1,128)S(1)}, u32[]{:S(2)}, u32[]{:S(2)}) collective-permute-start(f32[2,1,1]{0,2,1:T(1,128)S(1)} %get-tuple-element.19), channel_id=1, source_target_pairs={{0,448},{8,456},{16,464},{24,472},{32,480},{40,488},{48,496},{56,5... | collective-permute-start | bytes 32 | tf_op jit(solution)/shard_map/ppermute | solution.py:14
  158.8 6.7 %collective-permute-start.5 = (f32[2,3,2048]{2,0,1:T(2,128)S(1)}, f32[2,3,2048]{2,0,1:T(2,128)S(1)}, u32[]{:S(2)}, u32[]{:S(2)}) collective-permute-start(f32[2,3,2048]{2,0,1:T(2,128)S(1)} %pad_maximum_fusion.2), channel_id=1, source_target_pairs={{0,504},{8,0},{16,8},{24,16},{32,24},{40,32},{48,40},{56,48},{64,5... | collective-permute-start | bytes 147464 | tf_op jit(solution)/shard_map/ppermute | solution.py:14
  169.8 5.6 %collective-permute-start.48 = (f32[2,1,1]{0,2,1:T(1,128)S(1)}, f32[2,1,1]{0,2,1:T(1,128)S(1)}, u32[]{:S(2)}, u32[]{:S(2)}) collective-permute-start(f32[2,1,1]{0,2,1:T(1,128)S(1)} %get-tuple-element.13), channel_id=1, source_target_pairs={{0,384},{8,392},{16,400},{24,408},{32,416},{40,424},{48,432},{56,4... | collective-permute-start | bytes 32 | tf_op jit(solution)/shard_map/ppermute | solution.py:14
  185.0 5.5 %collective-permute-start.41 = (f32[2,1,1]{0,2,1:T(1,128)S(1)}, f32[2,1,1]{0,2,1:T(1,128)S(1)}, u32[]{:S(2)}, u32[]{:S(2)}) collective-permute-start(f32[2,1,1]{0,2,1:T(1,128)S(1)} %get-tuple-element.15), channel_id=1, source_target_pairs={{0,128},{8,136},{16,144},{24,152},{32,160},{40,168},{48,176},{56,1... | collective-permute-start | bytes 32 | tf_op jit(solution)/shard_map/ppermute | solution.py:14
  193.8 4.3 %collective-permute-start.18 = (f32[2,3,2048]{2,0,1:T(2,128)S(1)}, f32[2,3,2048]{2,0,1:T(2,128)S(1)}, u32[]{:S(2)}, u32[]{:S(2)}) collective-permute-start(f32[2,3,2048]{2,0,1:T(2,128)S(1)} %multiply_subtract_fusion.5), channel_id=1, source_target_pairs={{0,16},{8,24},{16,32},{24,40},{32,48},{40,56},{48,64},{56,72},{64,... | collective-permute-start | bytes 147464 | tf_op jit(solution)/shard_map/ppermute | solution.py:14
  198.2 5.6 %collective-permute-start.44 = (f32[2,1,1]{0,2,1:T(1,128)S(1)}, f32[2,1,1]{0,2,1:T(1,128)S(1)}, u32[]{:S(2)}, u32[]{:S(2)}) collective-permute-start(f32[2,1,1]{0,2,1:T(1,128)S(1)} %get-tuple-element.15), channel_id=1, source_target_pairs={{0,384},{8,392},{16,400},{24,408},{32,416},{40,424},{48,432},{56,4... | collective-permute-start | bytes 32 | tf_op jit(solution)/shard_map/ppermute | solution.py:14
  212.9 5.5 %collective-permute-start.51 = (f32[2,1,1]{0,2,1:T(1,128)S(1)}, f32[2,1,1]{0,2,1:T(1,128)S(1)}, u32[]{:S(2)}, u32[]{:S(2)}) collective-permute-start(f32[2,1,1]{0,2,1:T(1,128)S(1)} %negate_multiply_fusion.2), channel_id=1, source_target_pairs={{0,384},{8,392},{16,400},{24,408},{32,416},{40,424},{48,432},{56,4... | collective-permute-start | bytes 32 | tf_op jit(solution)/shard_map/ppermute | solution.py:14
  227.5 5.4 %collective-permute-start.45 = (f32[2,3,2048]{2,0,1:T(2,128)S(1)}, f32[2,3,2048]{2,0,1:T(2,128)S(1)}, u32[]{:S(2)}, u32[]{:S(2)}) collective-permute-start(f32[2,3,2048]{2,0,1:T(2,128)S(1)} %multiply_subtract_fusion.2), channel_id=1, source_target_pairs={{0,384},{8,392},{16,400},{24,408},{32,416},{40,424},{48,432},{56,4... | collective-permute-start | bytes 147464 | tf_op jit(solution)/shard_map/ppermute | solution.py:14
  236.8 7.2 %collective-permute-start.53 = (f32[2,1,1]{0,2,1:T(1,128)S(1)}, f32[2,1,1]{0,2,1:T(1,128)S(1)}, u32[]{:S(2)}, u32[]{:S(2)}) collective-permute-start(f32[2,1,1]{0,2,1:T(1,128)S(1)} %negate_multiply_fusion), channel_id=1, source_target_pairs={{0,256},{8,264},{16,272},{24,280},{32,288},{40,296},{48,304},{56,3... | collective-permute-start | bytes 32 | tf_op jit(solution)/shard_map/ppermute | solution.py:14
  244.0 6.8 %collective-permute-start.52 = (f32[2,1,1]{0,2,1:T(1,128)S(1)}, f32[2,1,1]{0,2,1:T(1,128)S(1)}, u32[]{:S(2)}, u32[]{:S(2)}) collective-permute-start(f32[2,1,1]{0,2,1:T(1,128)S(1)} %get-tuple-element.9), channel_id=1, source_target_pairs={{0,256},{8,264},{16,272},{24,280},{32,288},{40,296},{48,304},{56,3... | collective-permute-start | bytes 32 | tf_op jit(solution)/shard_map/ppermute | solution.py:14
  250.8 7.2 %collective-permute-start.49 = (f32[2,1,1]{0,2,1:T(1,128)S(1)}, f32[2,1,1]{0,2,1:T(1,128)S(1)}, u32[]{:S(2)}, u32[]{:S(2)}) collective-permute-start(f32[2,1,1]{0,2,1:T(1,128)S(1)} %get-tuple-element.11), channel_id=1, source_target_pairs={{0,256},{8,264},{16,272},{24,280},{32,288},{40,296},{48,304},{56,3... | collective-permute-start | bytes 32 | tf_op jit(solution)/shard_map/ppermute | solution.py:14
  258.1 6.8 %collective-permute-start.50 = (f32[2,3,2048]{2,0,1:T(2,128)S(1)}, f32[2,3,2048]{2,0,1:T(2,128)S(1)}, u32[]{:S(2)}, u32[]{:S(2)}) collective-permute-start(f32[2,3,2048]{2,0,1:T(2,128)S(1)} %multiply_subtract_fusion.1), channel_id=1, source_target_pairs={{0,256},{8,264},{16,272},{24,280},{32,288},{40,296},{48,304},{56,3... | collective-permute-start | bytes 147464 | tf_op jit(solution)/shard_map/ppermute | solution.py:14
  265.0 7.3 %collective-permute-done.50 = f32[2,3,2048]{2,0,1:T(2,128)S(1)} collective-permute-done((f32[2,3,2048]{2,0,1:T(2,128)S(1)}, f32[2,3,2048]{2,0,1:T(2,128)S(1)}, u32[]{:S(2)}, u32[]{:S(2)}) %collective-permute-start.50) | collective-permute-done | bytes 49184 | tf_op jit(solution)/shard_map/ppermute | solution.py:14
  274.8 122.5 %psum.7 = f32[]{:T(128)} all-reduce(f32[]{:T(128)} %get-tuple-element.4), channel_id=1, replica_groups=mesh['gx'=64,'yz'=8] {'gx','yz'}, use_global_device_ids=true, to_apply=%region_1.0 | all-reduce | flops 1 | bytes 8 | tf_op jit(solution)/shard_map/psum | solution.py:98
  (156 shorter events, 128.4 us)
Async XLA Ops:
  3.4 57.6 %collective-permute-start.7 = (f32[2,1,1]{2,1,0:T(1,128)}, f32[2,1,1]{2,1,0:T(1,128)}, u32[]{:S(2)}, u32[]{:S(2)}) collective-permute-start(f32[2,1,1]{2,1,0:T(1,128)} %copy.21), channel_id=1, source_target_pairs={{0,8},{8,16},{16,24},{24,32},{32,40},{40,48},{48,56},{56,64},{64,7... | collective-permute-start | bytes 32 | tf_op jit(solution)/shard_map/ppermute | solution.py:14
  7.4 65.1 %collective-permute-start.11 = (f32[2,1,1]{2,1,0:T(1,128)}, f32[2,1,1]{2,1,0:T(1,128)}, u32[]{:S(2)}, u32[]{:S(2)}) collective-permute-start(f32[2,1,1]{2,1,0:T(1,128)} %copy.21), channel_id=1, source_target_pairs={{0,504},{8,0},{16,8},{24,16},{32,24},{40,32},{48,40},{56,48},{64,5... | collective-permute-start | bytes 32 | tf_op jit(solution)/shard_map/ppermute | solution.py:14
  20.8 131.5 %collective-permute-start.1 = (f32[3,2,2048]{2,1,0:T(2,128)S(1)}, f32[3,2,2048]{2,1,0:T(2,128)S(1)}, u32[]{:S(2)}, u32[]{:S(2)}) collective-permute-start(f32[3,2,2048]{2,1,0:T(2,128)S(1)} %get-tuple-element.36), channel_id=1, source_target_pairs={{0,8},{8,16},{16,24},{24,32},{32,40},{40,48},{48,56},{56,64},{64,7... | collective-permute-start | bytes 147464 | tf_op jit(solution)/shard_map/ppermute | solution.py:23
  31.9 34.8 %collective-permute-start.8 = (f32[2,1,1]{0,2,1:T(1,128)}, f32[2,1,1]{0,2,1:T(1,128)}, u32[]{:S(2)}, u32[]{:S(2)}) collective-permute-start(f32[2,1,1]{0,2,1:T(1,128)} %fusion.17), channel_id=1, source_target_pairs={{0,504},{8,0},{16,8},{24,16},{32,24},{40,32},{48,40},{56,48},{64,5... | collective-permute-start | bytes 32 | tf_op jit(solution)/shard_map/ppermute | solution.py:14
  52.2 94.6 %collective-permute-start = (f32[3,2,2048]{2,1,0:T(2,128)S(1)}, f32[3,2,2048]{2,1,0:T(2,128)S(1)}, u32[]{:S(2)}, u32[]{:S(2)}) collective-permute-start(f32[3,2,2048]{2,1,0:T(2,128)S(1)} %get-tuple-element.35), channel_id=1, source_target_pairs={{8,0},{16,8},{24,16},{32,24},{40,32},{48,40},{56,48},{64,56},{72,6... | collective-permute-start | bytes 147464 | tf_op jit(solution)/shard_map/ppermute | solution.py:26
  61.0 27.1 %collective-permute-start.16 = (f32[2,1,1]{0,2,1:T(1,128)}, f32[2,1,1]{0,2,1:T(1,128)}, u32[]{:S(2)}, u32[]{:S(2)}) collective-permute-start(f32[2,1,1]{0,2,1:T(1,128)} %get-tuple-element.29), channel_id=1, source_target_pairs={{0,504},{8,0},{16,8},{24,16},{32,24},{40,32},{48,40},{56,48},{64,5... | collective-permute-start | bytes 32 | tf_op jit(solution)/shard_map/ppermute | solution.py:14
  79.9 16.8 %collective-permute-start.12 = (f32[2,1,1]{0,2,1:T(1,128)}, f32[2,1,1]{0,2,1:T(1,128)S(1)}, u32[]{:S(2)}, u32[]{:S(2)}) collective-permute-start(f32[2,1,1]{0,2,1:T(1,128)} %get-tuple-element.31), channel_id=1, source_target_pairs={{0,504},{8,0},{16,8},{24,16},{32,24},{40,32},{48,40},{56,48},{64,5... | collective-permute-start | bytes 32 | tf_op jit(solution)/shard_map/ppermute | solution.py:14
  94.8 18.3 %collective-permute-start.24 = (f32[2,1,1]{0,2,1:T(1,128)S(1)}, f32[2,1,1]{0,2,1:T(1,128)S(1)}, u32[]{:S(2)}, u32[]{:S(2)}) collective-permute-start(f32[2,1,1]{0,2,1:T(1,128)S(1)} %get-tuple-element.25), channel_id=1, source_target_pairs={{0,496},{8,504},{16,0},{24,8},{32,16},{40,24},{48,32},{56,40},{64,... | collective-permute-start | bytes 32 | tf_op jit(solution)/shard_map/ppermute | solution.py:14
  104.6 17.4 %collective-permute-start.20 = (f32[2,1,1]{0,2,1:T(1,128)S(1)}, f32[2,1,1]{0,2,1:T(1,128)S(1)}, u32[]{:S(2)}, u32[]{:S(2)}) collective-permute-start(f32[2,1,1]{0,2,1:T(1,128)S(1)} %get-tuple-element.27), channel_id=1, source_target_pairs={{0,496},{8,504},{16,0},{24,8},{32,16},{40,24},{48,32},{56,40},{64,... | collective-permute-start | bytes 32 | tf_op jit(solution)/shard_map/ppermute | solution.py:14
  138.6 37.0 %collective-permute-start.40 = (f32[2,1,1]{0,2,1:T(1,128)S(1)}, f32[2,1,1]{0,2,1:T(1,128)S(1)}, u32[]{:S(2)}, u32[]{:S(2)}) collective-permute-start(f32[2,1,1]{0,2,1:T(1,128)S(1)} %get-tuple-element.17), channel_id=1, source_target_pairs={{0,448},{8,456},{16,464},{24,472},{32,480},{40,488},{48,496},{56,5... | collective-permute-start | bytes 32 | tf_op jit(solution)/shard_map/ppermute | solution.py:14
  140.5 16.3 %collective-permute-start.38 = (f32[2,1,1]{0,2,1:T(1,128)S(1)}, f32[2,1,1]{0,2,1:T(1,128)S(1)}, u32[]{:S(2)}, u32[]{:S(2)}) collective-permute-start(f32[2,1,1]{0,2,1:T(1,128)S(1)} %get-tuple-element.17), channel_id=1, source_target_pairs={{0,64},{8,72},{16,80},{24,88},{32,96},{40,104},{48,112},{56,120},{... | collective-permute-start | bytes 32 | tf_op jit(solution)/shard_map/ppermute | solution.py:14
  146.8 36.2 %collective-permute-start.36 = (f32[2,1,1]{0,2,1:T(1,128)S(1)}, f32[2,1,1]{0,2,1:T(1,128)S(1)}, u32[]{:S(2)}, u32[]{:S(2)}) collective-permute-start(f32[2,1,1]{0,2,1:T(1,128)S(1)} %get-tuple-element.19), channel_id=1, source_target_pairs={{0,448},{8,456},{16,464},{24,472},{32,480},{40,488},{48,496},{56,5... | collective-permute-start | bytes 32 | tf_op jit(solution)/shard_map/ppermute | solution.py:14
  152.3 26.9 %collective-permute-start.39 = (f32[2,1,1]{0,2,1:T(1,128)S(1)}, f32[2,1,1]{0,2,1:T(1,128)S(1)}, u32[]{:S(2)}, u32[]{:S(2)}) collective-permute-start(f32[2,1,1]{0,2,1:T(1,128)S(1)} %negate_multiply_fusion.4), channel_id=1, source_target_pairs={{0,64},{8,72},{16,80},{24,88},{32,96},{40,104},{48,112},{56,120},{... | collective-permute-start | bytes 32 | tf_op jit(solution)/shard_map/ppermute | solution.py:14
  165.5 28.3 %collective-permute-start.43 = (f32[2,1,1]{0,2,1:T(1,128)S(1)}, f32[2,1,1]{0,2,1:T(1,128)S(1)}, u32[]{:S(2)}, u32[]{:S(2)}) collective-permute-start(f32[2,1,1]{0,2,1:T(1,128)S(1)} %negate_multiply_fusion.4), channel_id=1, source_target_pairs={{0,448},{8,456},{16,464},{24,472},{32,480},{40,488},{48,496},{56,5... | collective-permute-start | bytes 32 | tf_op jit(solution)/shard_map/ppermute | solution.py:14
  169.8 50.7 %collective-permute-start.48 = (f32[2,1,1]{0,2,1:T(1,128)S(1)}, f32[2,1,1]{0,2,1:T(1,128)S(1)}, u32[]{:S(2)}, u32[]{:S(2)}) collective-permute-start(f32[2,1,1]{0,2,1:T(1,128)S(1)} %get-tuple-element.13), channel_id=1, source_target_pairs={{0,384},{8,392},{16,400},{24,408},{32,416},{40,424},{48,432},{56,4... | collective-permute-start | bytes 32 | tf_op jit(solution)/shard_map/ppermute | solution.py:14
  175.6 32.0 %collective-permute-start.46 = (f32[2,1,1]{0,2,1:T(1,128)S(1)}, f32[2,1,1]{0,2,1:T(1,128)S(1)}, u32[]{:S(2)}, u32[]{:S(2)}) collective-permute-start(f32[2,1,1]{0,2,1:T(1,128)S(1)} %get-tuple-element.13), channel_id=1, source_target_pairs={{0,128},{8,136},{16,144},{24,152},{32,160},{40,168},{48,176},{56,1... | collective-permute-start | bytes 32 | tf_op jit(solution)/shard_map/ppermute | solution.py:14
  185.0 24.5 %collective-permute-start.41 = (f32[2,1,1]{0,2,1:T(1,128)S(1)}, f32[2,1,1]{0,2,1:T(1,128)S(1)}, u32[]{:S(2)}, u32[]{:S(2)}) collective-permute-start(f32[2,1,1]{0,2,1:T(1,128)S(1)} %get-tuple-element.15), channel_id=1, source_target_pairs={{0,128},{8,136},{16,144},{24,152},{32,160},{40,168},{48,176},{56,1... | collective-permute-start | bytes 32 | tf_op jit(solution)/shard_map/ppermute | solution.py:14
  198.2 26.6 %collective-permute-start.44 = (f32[2,1,1]{0,2,1:T(1,128)S(1)}, f32[2,1,1]{0,2,1:T(1,128)S(1)}, u32[]{:S(2)}, u32[]{:S(2)}) collective-permute-start(f32[2,1,1]{0,2,1:T(1,128)S(1)} %get-tuple-element.15), channel_id=1, source_target_pairs={{0,384},{8,392},{16,400},{24,408},{32,416},{40,424},{48,432},{56,4... | collective-permute-start | bytes 32 | tf_op jit(solution)/shard_map/ppermute | solution.py:14
  203.8 21.0 %collective-permute-start.47 = (f32[2,1,1]{0,2,1:T(1,128)S(1)}, f32[2,1,1]{0,2,1:T(1,128)S(1)}, u32[]{:S(2)}, u32[]{:S(2)}) collective-permute-start(f32[2,1,1]{0,2,1:T(1,128)S(1)} %negate_multiply_fusion.2), channel_id=1, source_target_pairs={{0,128},{8,136},{16,144},{24,152},{32,160},{40,168},{48,176},{56,1... | collective-permute-start | bytes 32 | tf_op jit(solution)/shard_map/ppermute | solution.py:14
  212.9 23.8 %collective-permute-start.51 = (f32[2,1,1]{0,2,1:T(1,128)S(1)}, f32[2,1,1]{0,2,1:T(1,128)S(1)}, u32[]{:S(2)}, u32[]{:S(2)}) collective-permute-start(f32[2,1,1]{0,2,1:T(1,128)S(1)} %negate_multiply_fusion.2), channel_id=1, source_target_pairs={{0,384},{8,392},{16,400},{24,408},{32,416},{40,424},{48,432},{56,4... | collective-permute-start | bytes 32 | tf_op jit(solution)/shard_map/ppermute | solution.py:14
  227.5 30.5 %collective-permute-start.45 = (f32[2,3,2048]{2,0,1:T(2,128)S(1)}, f32[2,3,2048]{2,0,1:T(2,128)S(1)}, u32[]{:S(2)}, u32[]{:S(2)}) collective-permute-start(f32[2,3,2048]{2,0,1:T(2,128)S(1)} %multiply_subtract_fusion.2), channel_id=1, source_target_pairs={{0,384},{8,392},{16,400},{24,408},{32,416},{40,424},{48,432},{56,4... | collective-permute-start | bytes 147464 | tf_op jit(solution)/shard_map/ppermute | solution.py:14
  233.0 25.0 %collective-permute-start.42 = (f32[2,3,2048]{2,0,1:T(2,128)S(1)}, f32[2,3,2048]{2,0,1:T(2,128)S(1)}, u32[]{:S(2)}, u32[]{:S(2)}) collective-permute-start(f32[2,3,2048]{2,0,1:T(2,128)S(1)} %multiply_subtract_fusion.2), channel_id=1, source_target_pairs={{0,128},{8,136},{16,144},{24,152},{32,160},{40,168},{48,176},{56,1... | collective-permute-start | bytes 147464 | tf_op jit(solution)/shard_map/ppermute | solution.py:14
  236.8 28.2 %collective-permute-start.53 = (f32[2,1,1]{0,2,1:T(1,128)S(1)}, f32[2,1,1]{0,2,1:T(1,128)S(1)}, u32[]{:S(2)}, u32[]{:S(2)}) collective-permute-start(f32[2,1,1]{0,2,1:T(1,128)S(1)} %negate_multiply_fusion), channel_id=1, source_target_pairs={{0,256},{8,264},{16,272},{24,280},{32,288},{40,296},{48,304},{56,3... | collective-permute-start | bytes 32 | tf_op jit(solution)/shard_map/ppermute | solution.py:14
  244.0 20.9 %collective-permute-start.52 = (f32[2,1,1]{0,2,1:T(1,128)S(1)}, f32[2,1,1]{0,2,1:T(1,128)S(1)}, u32[]{:S(2)}, u32[]{:S(2)}) collective-permute-start(f32[2,1,1]{0,2,1:T(1,128)S(1)} %get-tuple-element.9), channel_id=1, source_target_pairs={{0,256},{8,264},{16,272},{24,280},{32,288},{40,296},{48,304},{56,3... | collective-permute-start | bytes 32 | tf_op jit(solution)/shard_map/ppermute | solution.py:14
  (33 other events, 427.0 us)
where the time goes:
time: 401 us; the launch traced here: 399 us
  starting transfers between devices  218 us (54%)
  blocking collectives  123 us (31%)
  waiting for transfers between devices  19.9 us (5%)
  other arithmetic  16.4 us (4%)
  local copies, waits for them, and re-layouts  14.6 us (4%)
  between operations  5.83 us (1%)
    ppermute x52, starting transfers between devices, passed_along(): return lax.ppermute(value, axis, pairs)  214 us
    psum x1, blocking collectives, on_device(): energy_sum = lax.psum(jnp.sum(derivative * derivative), ('gx', 'yz'))  123 us
    ppermute x52, waiting for transfers between devices, passed_along(): return lax.ppermute(value, axis, pairs)  19.9 us
  transfers between devices with their start and end apart: 54, of which 7 were waited for; matrix products, arithmetic and copies ran while one was open for 7% of the time, Pallas kernels for 0%

commit v1 on v0

v1 whole, which is shorter than its diff:
```python
import functools

import jax
import jax.numpy as jnp
from jax import lax
from jax.experimental import pallas as pl
from jax.experimental.pallas import tpu as pltpu
from jax.sharding import PartitionSpec as P

COUPLING = 1.0 / 3.0
NEAR_WEIGHT = 7.0 / 9.0
FAR_WEIGHT = 1.0 / 36.0

GROUP = 16
GROUPS = 4
LANES = 128
CELLS = 64
F32 = jnp.float32


def lane_row(value, lanes=LANES):
    return jnp.broadcast_to(value, (1, lanes))


def tiled(value, copies):
    return jnp.concatenate([value] * copies, axis=1)


def local_kernel(v_ref, block_ref, g_ref, send_ref, p_ref, q_ref, mat_ref, pad_ref, energy_ref):
    comp = pl.program_id(0)
    inner = CELLS - 2
    lines = v_ref.shape[2]
    row8 = lax.broadcasted_iota(jnp.int32, (8, lines), 0)

    @pl.when(comp == 0)
    def _():
        pad_ref[...] = jnp.zeros(pad_ref.shape, F32)
        pad_ref[0:inner, 0:inner] = block_ref[0]
        padded = pltpu.roll(pltpu.roll(pad_ref[...], 1, 0), 1, 1)
        first = jnp.broadcast_to(COUPLING * padded[:, 1:2], (CELLS, LANES))
        last = jnp.broadcast_to(COUPLING * padded[:, inner : inner + 1], (CELLS, LANES))
        p_ref[...] = first
        q_ref[...] = last
        cols = lax.broadcasted_iota(jnp.int32, (1, LANES), 1)
        top = jnp.where(cols == 0, 1.0, 0.0) - COUPLING * padded[1:2]
        bottom = jnp.where(cols == CELLS - 1, 1.0, 0.0) - COUPLING * padded[inner : inner + 1]
        first_sum = jnp.sum(first * padded, axis=0, keepdims=True)
        last_sum = jnp.sum(last * padded, axis=0, keepdims=True)
        mat_ref[0:CELLS, :] = padded
        rows = lax.broadcasted_iota(jnp.int32, (8, LANES), 0)
        extra = jnp.where(rows == 0, top, 0.0)
        extra = jnp.where(rows == 1, bottom, extra)
        extra = jnp.where(rows == 2, first_sum, extra)
        extra = jnp.where(rows == 3, last_sum, extra)
        mat_ref[CELLS : CELLS + 8, :] = extra
        energy_ref[...] = jnp.zeros(energy_ref.shape, F32)

    v = v_ref[0]
    low, high = v[0:1], v[CELLS - 1 : CELLS]
    below_1 = jnp.concatenate([low, v[: CELLS - 1]], 0)
    below_2 = jnp.concatenate([low, low, v[: CELLS - 2]], 0)
    above_1 = jnp.concatenate([v[1:], high], 0)
    above_2 = jnp.concatenate([v[2:], high, high], 0)
    right = NEAR_WEIGHT * (above_1 - below_1) + FAR_WEIGHT * (above_2 - below_2)
    out = jnp.dot(
        mat_ref[:, 0:CELLS], right, precision=lax.Precision.HIGHEST, preferred_element_type=F32
    )
    g = out[0:CELLS]
    g_ref[0] = g
    squares = jnp.sum(g * g, axis=0, keepdims=True)
    part = squares[:, 0:LANES]
    for j in range(1, GROUP):
        part = part + squares[:, j * LANES : (j + 1) * LANES]
    energy_ref[0:1, :] += part
    rows = out[CELLS : CELLS + 8]
    rows = jnp.where((row8 == 4) | (row8 == 5), pltpu.roll(v[0:8], 4, 0), rows)
    rows = jnp.where(row8 >= 6, v[CELLS - 8 : CELLS], rows)
    at = pl.multiple_of(comp * 8, 8)
    for j in range(GROUP):
        send_ref[j, pl.ds(at, 8), :] = rows[:, j * LANES : (j + 1) * LANES]

    @pl.when(comp == pl.num_programs(0) - 1)
    def _():
        first, last = p_ref[...], q_ref[...]
        coefs = jnp.concatenate(
            [
                first[1:2],
                last[1:2],
                first[inner : inner + 1],
                last[inner : inner + 1],
                jnp.sum(first * first, axis=0, keepdims=True),
                jnp.sum(first * last, axis=0, keepdims=True),
                jnp.sum(last * last, axis=0, keepdims=True),
                energy_ref[0:1, :],
            ],
            0,
        )
        for j in range(GROUP):
            send_ref[j, send_ref.shape[1] - 8 :, :] = coefs


def group_kernel(recv_ref, msg_ref, state_ref, open_ref):
    stride = recv_ref.shape[0] // GROUP
    comps = stride // 8 - 1
    width = comps * LANES

    def rows(r):
        parts = [recv_ref[pl.ds(8 * i + r, GROUP, stride=stride), :] for i in range(comps)]
        return jnp.concatenate(parts, 1)

    def coef(r):
        return recv_ref[pl.ds(8 * comps + r, GROUP, stride=stride), :]

    seg = lax.broadcasted_iota(jnp.int32, (GROUP, width), 0)
    seg_1 = lax.broadcasted_iota(jnp.int32, (GROUP, LANES), 0)

    def prev(x, s=1):
        return pltpu.roll(x, s, 0)

    def following(x, s=1):
        return pltpu.roll(x, GROUP - s, 0)

    b_first, b_last, pg, qg, v_0, v_1, v_62, v_63 = [rows(r) for r in range(8)]
    p_0, q_0, p_61, q_61, pp, pq, qq, energy = [coef(r) for r in range(8)]
    jump_l = jnp.where(seg == 0, 0.0, prev(v_63) - v_0)
    jump_l2 = jnp.where(seg == 0, 0.0, prev(v_62) - v_0)
    jump_r = jnp.where(seg == GROUP - 1, 0.0, v_63 - following(v_0))
    jump_r2 = jnp.where(seg == GROUP - 1, 0.0, following(v_1) - v_63)
    b_first = b_first - (2.0 / 3.0) * jump_l - FAR_WEIGHT * jump_l2
    b_last = b_last - (2.0 / 3.0) * jump_r + FAR_WEIGHT * jump_r2

    unit_first = jnp.where(seg_1 == 0, 1.0, 0.0)
    unit_last = jnp.where(seg_1 == GROUP - 1, 1.0, 0.0)
    zero = jnp.zeros((GROUP, LANES), F32)
    third = jnp.full((GROUP, LANES), COUPLING, F32)
    rhs_f = jnp.concatenate([b_first, unit_first, zero], 1)
    rhs_l = jnp.concatenate([b_last, zero, unit_last], 1)
    f = (jnp.where(seg_1 == 0, 0.0, third), 1.0 - COUPLING * p_0, -COUPLING * q_0, rhs_f)
    l = (-COUPLING * p_61, 1.0 - COUPLING * q_61, jnp.where(seg_1 == GROUP - 1, 0.0, third), rhs_l)

    def reduce_level(mine, below, above):
        ratio_low = mine[0] / below[1]
        ratio_high = mine[2] / above[1]
        return (
            -ratio_low * below[0],
            mine[1] - ratio_low * below[2] - ratio_high * above[0],
            -ratio_high * above[2],
            mine[3] - tiled(ratio_low, comps + 2) * below[3] - tiled(ratio_high, comps + 2) * above[3],
        )

    f, l = (
        reduce_level(f, tuple(prev(x) for x in l), l),
        reduce_level(l, f, tuple(following(x) for x in f)),
    )
    step = 1
    while step < GROUP:
        f = reduce_level(f, tuple(prev(x, step) for x in f), tuple(following(x, step) for x in f))
        l = reduce_level(l, tuple(prev(x, step) for x in l), tuple(following(x, step) for x in l))
        step *= 2
    sol_f = f[3] / tiled(f[1], comps + 2)
    sol_l = l[3] / tiled(l[1], comps + 2)
    x_f, a_f, c_f = sol_f[:, :width], sol_f[:, width : width + LANES], sol_f[:, width + LANES :]
    x_l, a_l, c_l = sol_l[:, :width], sol_l[:, width : width + LANES], sol_l[:, width + LANES :]

    pp1, qq1 = pp + 1.0, qq + 1.0
    d_l, d_r = jump_l * (1.0 / 12.0), jump_r * (1.0 / 12.0)
    pq_w = tiled(pq, comps)
    m_f = tiled(pp1, comps) * x_f + pq_w * x_l - pg - d_l
    m_l = tiled(qq1, comps) * x_l + pq_w * x_f - qg - d_r

    def total(x):
        return jnp.sum(x, axis=0, keepdims=True)

    line_a = 2.0 * total(tiled(a_f, comps) * m_f + tiled(a_l, comps) * m_l)
    line_c = 2.0 * total(tiled(c_f, comps) * m_f + tiled(c_l, comps) * m_l)
    base = total(x_f * (m_f - pg - d_l) + x_l * (m_l - qg - d_r) + d_l * d_l + d_r * d_r)
    part = total(energy) * (1.0 / GROUP)
    for i in range(comps):
        part = part + base[:, i * LANES : (i + 1) * LANES]
    quad_aa = total(pp1 * a_f * a_f + 2.0 * pq * a_f * a_l + qq1 * a_l * a_l)
    quad_ac = total(pp1 * a_f * c_f + pq * (a_f * c_l + a_l * c_f) + qq1 * a_l * c_l)
    quad_cc = total(pp1 * c_f * c_f + 2.0 * pq * c_f * c_l + qq1 * c_l * c_l)

    end = GROUP - 1
    msg_ref[:, 0:width] = jnp.concatenate(
        [x_f[0:1], x_l[end:], line_a, line_c, v_0[0:1], v_1[0:1], v_62[end:], v_63[end:]], 0
    )
    msg_ref[:, width : width + LANES] = jnp.concatenate(
        [a_f[0:1], a_l[end:], c_f[0:1], c_l[end:], quad_aa, quad_ac, quad_cc, part], 0
    )
    state_ref[0] = x_f
    state_ref[1] = x_l
    state_ref[2] = jump_l
    state_ref[3] = jump_r
    open_ref[0] = a_f
    open_ref[1] = a_l
    open_ref[2] = c_f
    open_ref[3] = c_l


def eliminate(matrix, rhs, wide):
    size = len(rhs)
    matrix = [list(r) for r in matrix]
    rhs = list(rhs)
    inverse = [None] * size
    for k in range(size):
        inverse[k] = 1.0 / matrix[k][k]
        for i in range(k + 1, size):
            if matrix[i][k] is None:
                continue
            ratio = matrix[i][k] * inverse[k]
            for j in range(k + 1, size):
                if matrix[k][j] is not None:
                    old = matrix[i][j]
                    change = ratio * matrix[k][j]
                    matrix[i][j] = -change if old is None else old - change
            rhs[i] = rhs[i] - wide(ratio) * rhs[k]
    found = [None] * size
    for k in reversed(range(size)):
        value = rhs[k]
        for j in range(k + 1, size):
            if matrix[k][j] is not None:
                value = value - wide(matrix[k][j]) * found[j]
        found[k] = value * wide(inverse[k])
    return found


def join_kernel(own_ref, near_ref, far_ref, state_ref, open_ref, send_ref, all_ref):
    width = state_ref.shape[2]
    comps = width // LANES
    group = lax.axis_index("gx") // GROUP
    all_ref[0] = own_ref[...]
    all_ref[1] = near_ref[...]
    all_ref[2] = far_ref[1]
    all_ref[3] = far_ref[0]

    def wide(x):
        return tiled(x, comps)

    tile = []
    for t in range(GROUPS):
        own = group % 4
        slot = jnp.where(own >= 2, (t // 2) ^ 1, t // 2) * 2 + jnp.where(own % 2 == 1, (t % 2) ^ 1, t % 2)
        tile.append(all_ref[slot])
    data = [[m[r : r + 1, 0:width] for r in range(8)] for m in tile]
    scal = [[m[r : r + 1, width:] for r in range(8)] for m in tile]
    x_f, x_l, line_a, line_c, v_0, v_1, v_62, v_63 = [[d[r] for d in data] for r in range(8)]
    a_f, a_l, c_f, c_l, q_aa, q_ac, q_cc, part = [[s[r] for s in scal] for r in range(8)]

    one = jnp.ones((1, LANES), F32)
    jump = [v_63[t - 1] - v_0[t] for t in range(GROUPS)]
    matrix, rhs = [], []
    for t in range(GROUPS):
        before, after = (t - 1) % GROUPS, (t + 1) % GROUPS
        row_a, row_c = [None] * (2 * GROUPS), [None] * (2 * GROUPS)
        row_a[2 * t] = one
        row_a[2 * before] = COUPLING * a_l[before]
        row_a[2 * before + 1] = COUPLING * c_l[before]
        row_c[2 * t + 1] = one
        row_c[2 * after] = COUPLING * a_f[after]
        row_c[2 * after + 1] = COUPLING * c_f[after]
        matrix += [row_a, row_c]
        rhs.append(
            -COUPLING * x_l[before] - (2.0 / 3.0) * jump[t] - FAR_WEIGHT * (v_62[before] - v_0[t])
        )
        rhs.append(
            -COUPLING * x_f[after] - (2.0 / 3.0) * jump[after] + FAR_WEIGHT * (v_1[after] - v_63[t])
        )
    found = eliminate(matrix, rhs, wide)
    value_a, value_c = found[0::2], found[1::2]

    energy = jnp.zeros((1, LANES), F32)
    for t in range(GROUPS):
        a, c = value_a[t], value_c[t]
        after = (t + 1) % GROUPS
        u_end = x_f[t] + wide(a_f[t]) * a + wide(c_f[t]) * c
        w_end = x_l[t] + wide(a_l[t]) * a + wide(c_l[t]) * c
        d_l, d_r = jump[t] * (1.0 / 12.0), jump[after] * (1.0 / 12.0)
        lines = a * (line_a[t] + wide(q_aa[t]) * a + wide(2.0 * q_ac[t]) * c)
        lines = lines + c * (line_c[t] + wide(q_cc[t]) * c)
        lines = lines + d_l * (d_l - 2.0 * u_end) + d_r * (d_r - 2.0 * w_end)
        energy = energy + part[t]
        for i in range(comps):
            energy = energy + lines[:, i * LANES : (i + 1) * LANES]

    def mine(values):
        result = values[0]
        for t in range(1, GROUPS):
            result = jnp.where(group == t, values[t], result)
        return result

    a, c = mine(value_a), mine(value_c)
    left, right = mine(jump), mine(jump[1:] + jump[:1])
    seg = lax.broadcasted_iota(jnp.int32, (GROUP, width), 0)
    u_t = state_ref[0] + wide(open_ref[0]) * a + wide(open_ref[2]) * c
    w_t = state_ref[1] + wide(open_ref[1]) * a + wide(open_ref[3]) * c
    jump_l = jnp.where(seg == 0, left, state_ref[2])
    jump_r = jnp.where(seg == GROUP - 1, right, state_ref[3])
    u = u_t - jump_l * (1.0 / 12.0)
    w = w_t - jump_r * (1.0 / 12.0)
    send_ref[...] = jnp.zeros(send_ref.shape, F32)
    for i in range(comps):
        for r, value in enumerate((u_t, w_t, u, w)):
            part_i = value[:, i * LANES : (i + 1) * LANES]
            send_ref[pl.ds(8 * i + r, GROUP, stride=8 * comps), :] = part_i
    send_ref[pl.ds(4, GROUP, stride=8 * comps), :] = jnp.broadcast_to(energy, (GROUP, LANES))


def final_kernel(recv_ref, g_ref, p_ref, q_ref, out_ref, energy_ref):
    row8 = lax.broadcasted_iota(jnp.int32, (8, LANES), 0)
    first, last = p_ref[...], q_ref[...]

    @pl.when(pl.program_id(0) == 0)
    def _():
        energy = recv_ref[0, 4:5, :]
        for j in range(1, GROUP):
            energy = energy + recv_ref[j, 4:5, :]
        energy_ref[...] = jnp.broadcast_to(energy, energy_ref.shape)

    for j in range(GROUP):
        at = slice(j * LANES, (j + 1) * LANES)
        u_t, w_t = recv_ref[j, 0:1, :], recv_ref[j, 1:2, :]
        u, w = recv_ref[j, 2:3, :], recv_ref[j, 3:4, :]
        value = g_ref[0, :, at] - first * u_t - last * w_t
        out_ref[0, 0:8, at] = jnp.where(row8 == 0, u, value[0:8])
        out_ref[0, 8 : CELLS - 8, at] = value[8 : CELLS - 8]
        out_ref[0, CELLS - 8 :, at] = jnp.where(row8 == 7, w, value[CELLS - 8 :])


def on_device(velocity, blocks):
    comps, cells, lines = velocity.shape
    width = comps * LANES
    yz_count = lax.axis_size("yz")
    groups = [[GROUP * t + i for i in range(GROUP)] for t in range(GROUPS)]
    shape = functools.partial(jax.ShapeDtypeStruct, dtype=F32)

    g, send, p_rows, q_rows = pl.pallas_call(
        local_kernel,
        grid=(comps,),
        in_specs=[
            pl.BlockSpec((1, cells, lines), lambda c: (c, 0, 0)),
            pl.BlockSpec(blocks.shape, lambda c: (0, 0, 0)),
        ],
        out_specs=[
            pl.BlockSpec((1, cells, lines), lambda c: (c, 0, 0)),
            pl.BlockSpec((GROUP, 8 * (comps + 1), LANES), lambda c: (0, 0, 0)),
            pl.BlockSpec((cells, LANES), lambda c: (0, 0)),
            pl.BlockSpec((cells, LANES), lambda c: (0, 0)),
        ],
        out_shape=[
            shape((comps, cells, lines)),
            shape((GROUP, 8 * (comps + 1), LANES)),
            shape((cells, LANES)),
            shape((cells, LANES)),
        ],
        scratch_shapes=[
            pltpu.VMEM((cells + 8, LANES), F32),
            pltpu.VMEM((cells, LANES), F32),
            pltpu.VMEM((8, LANES), F32),
        ],
        compiler_params=pltpu.CompilerParams(vmem_limit_bytes=32 * 1024 * 1024),
        name="local_solve",
    )(velocity, blocks)

    recv = lax.all_to_all(send, "gx", 0, 0, axis_index_groups=groups, tiled=True)
    msg, state, opened = pl.pallas_call(
        group_kernel,
        out_shape=[
            shape((8, width + LANES)),
            shape((4, GROUP, width)),
            shape((4, GROUP, LANES)),
        ],
        name="group_solve",
    )(recv.reshape(GROUP * 8 * (comps + 1), LANES))

    def swapped(value, mask):
        pairs = [
            (t * GROUP + i, (t ^ mask) * GROUP + i) for t in range(GROUPS) for i in range(GROUP)
        ]
        return lax.ppermute(value, "gx", pairs)

    near = swapped(msg, 1)
    far = swapped(jnp.stack([msg, near]), 3)
    send_back = pl.pallas_call(
        join_kernel,
        out_shape=shape((GROUP * 8 * comps, LANES)),
        scratch_shapes=[pltpu.VMEM((GROUPS, 8, width + LANES), F32)],
        name="join_groups",
    )(msg, near, far, state, opened)
    back = lax.all_to_all(
        send_back.reshape(GROUP, 8 * comps, LANES), "gx", 0, 0, axis_index_groups=groups, tiled=True
    )

    derivative, energy = pl.pallas_call(
        final_kernel,
        grid=(comps,),
        in_specs=[
            pl.BlockSpec((GROUP, 8, LANES), lambda c: (0, c, 0)),
            pl.BlockSpec((1, cells, lines), lambda c: (c, 0, 0)),
            pl.BlockSpec((cells, LANES), lambda c: (0, 0)),
            pl.BlockSpec((cells, LANES), lambda c: (0, 0)),
        ],
        out_specs=[
            pl.BlockSpec((1, cells, lines), lambda c: (c, 0, 0)),
            pl.BlockSpec((yz_count, LANES), lambda c: (0, 0)),
        ],
        out_shape=[shape((comps, cells, lines)), shape((yz_count, LANES))],
        compiler_params=pltpu.CompilerParams(vmem_limit_bytes=32 * 1024 * 1024),
        name="final_update",
    )(back, g, p_rows, q_rows)
    energies = lax.all_to_all(energy, "yz", 0, 0, tiled=True)
    total_count = comps * cells * lines * lax.axis_size("gx") * yz_count
    return derivative, jnp.sum(energies) / total_count


def solution(mesh):
    placed = (P(None, "gx", "yz"), P("gx", None, None))
    return jax.shard_map(
        on_device, mesh=mesh, in_specs=placed, out_specs=(P(None, "gx", "yz"), P()), check_vma=False
    )
```

time: 401 us -> 79.5 us (0.20)
  starting transfers between devices: 218 us -> 17.1 us
  blocking collectives: 123 us -> 44.7 us
  waiting for transfers between devices: 19.9 us -> 2.7 us
  other arithmetic: 16.4 us -> 1.34 us
  local copies, waits for them, and re-layouts: 14.6 us -> 2.77 us
  Pallas kernels: 0 us -> 7.81 us
    ppermute x54 -> x2, starting transfers between devices: 218 us -> 17.1 us  [swapped(): return lax.ppermute(value, 'gx', pairs)]
    psum x1 -> x0, blocking collectives: 123 us -> none  [on_device(): energy_sum = lax.psum(jnp.sum(derivative * derivative), ('gx', 'yz'))]
    all_to_all x0 -> x3, blocking collectives: none -> 44.7 us  [the longest x1 18.5 us: on_device(): lax.all_to_all(send, 'gx', 0, 0, axis_index_groups=groups, tiled=True)]
    ppermute x54 -> x2, waiting for transfers between devices: 19.9 us -> 2.7 us  [swapped(): return lax.ppermute(value, 'gx', pairs)]
    pallas_call x0 -> x4, Pallas kernels: none -> 7.81 us  [the longest x1 2.35 us: on_device(): pl.pallas_call(local_kernel, grid=(comps,), in_specs=[pl.BlockSpec((1, ce...]
    concatenate x5 -> x0, local copies, waits for them, and re-layouts: 5.12 us -> none  [the longest x3 3.82 us: doubling_solve(): jnp.concatenate([theirs[1:2], mine[0:1]], 0)]
    slice x8 -> x0, local copies, waits for them, and re-layouts: 5.03 us -> none  [the longest x4 2.23 us: doubling_solve(): theirs[1:2]]
    concatenate x4 -> x0, other arithmetic: 4.84 us -> none  [the longest x3 3.6 us: doubling_solve(): jnp.concatenate([theirs[1:2], mine[0:1]], 0)]
  transfers between devices with their start and end apart: 54 -> 2, of which waited for: 7 -> 2; matrix products, arithmetic and copies ran while one was open for 7% -> 0% of each run, Pallas kernels for 0% -> 0%
where the time goes in v1:
time: 79.5 us; the launch traced here: 78.9 us
  blocking collectives  44.7 us (56%)
  starting transfers between devices  17.1 us (22%)
  Pallas kernels  7.81 us (10%)
  local copies, waits for them, and re-layouts  2.77 us (3%)
  waiting for transfers between devices  2.7 us (3%)
  between operations  2.44 us (3%)
  other arithmetic  1.34 us (2%)
    all_to_all x1, blocking collectives, on_device(): lax.all_to_all(send, 'gx', 0, 0, axis_index_groups=groups, tiled=True)  18.5 us
    ppermute x2, starting transfers between devices, swapped(): return lax.ppermute(value, 'gx', pairs)  17.1 us
    all_to_all x1, blocking collectives, on_device(): energies = lax.all_to_all(energy, 'yz', 0, 0, tiled=True)  13.4 us
    all_to_all x1, blocking collectives, on_device(): lax.all_to_all(send_back.reshape(GROUP, 8 * comps, LANES), 'gx', 0, 0, ax...  12.9 us
    unnamed x7, local copies, waits for them, and re-layouts  2.77 us
    ppermute x2, waiting for transfers between devices, swapped(): return lax.ppermute(value, 'gx', pairs)  2.7 us
    pallas_call x1, Pallas kernels, on_device(): pl.pallas_call(local_kernel, grid=(comps,), in_specs=[pl.BlockSpec((1, ce...  2.35 us
    pallas_call x1, Pallas kernels, on_device(): pl.pallas_call(group_kernel, out_shape=[shape((8, width + LANES)), shape(...  1.87 us
  transfers between devices with their start and end apart: 2, of which 2 were waited for; matrix products, arithmetic and copies ran while one was open for 0% of the time, Pallas kernels for 0%

profile of v1, /device:TPU:1, one launch (start us, length us, event | category | flops | bytes accessed | tf_op | source)
XLA Modules:
  0.0 78.9 jit_solution(11083497061622851328)
XLA Ops:
  0.6 0.8 copy.5.block_ref
  1.4 0.0 copy-start
  1.4 1.4 %copy-done = f32[3,64,2048]{2,1,0:T(8,128)S(1)} copy-done((f32[3,64,2048]{2,1,0:T(8,128)S(1)}, f32[3,64,2048]{2,1,0:T(8,128)}, u32[]{:S(2)}) %copy-start) | copy-done | bytes 1572888
  2.8 2.4 %local_solve.1 = (f32[3,64,2048]{2,1,0:T(8,128)S(1)}, f32[16,32,128]{2,1,0:T(8,128)S(1)}, f32[64,128]{1,0:T(8,128)S(1)}, f32[64,128]{1,0:T(8,128)S(1)}) custom-call(f32[3,64,2048]{2,1,0:T(8,128)S(1)} %copy-done, f32[1,62,62]{2,1,0:T(8,128)S(1)} %copy.5.block_ref), custom_call_target="tpu_custom_call" | custom-call | tf_op jit(solution)/shard_map/local_solve/pallas_call | solution.py:337
  5.2 18.5 %all_to_all.19 = f32[16,32,128]{2,1,0:T(8,128)} all-to-all(f32[16,32,128]{2,1,0:T(8,128)S(1)} %get-tuple-element.11), channel_id=1, replica_groups={{0,8,16,24,32,40,48,56,64,72,80,88,96,104,112,120},{128,136,144,152,160..., dimensions={0} | all-to-all | bytes 524288 | tf_op jit(solution)/shard_map/all_to_all | solution.py:365
  23.6 1.9 %group_solve.1 = (f32[8,512]{1,0:T(8,128)}, f32[4,16,384]{2,1,0:T(8,128)}, f32[4,16,128]{2,1,0:T(8,128)}) custom-call(f32[512,128]{1,0:T(8,128)} %bitcast.8), custom_call_target="tpu_custom_call" | custom-call | tf_op jit(solution)/shard_map/group_solve/pallas_call | solution.py:366
  25.5 8.9 %collective-permute-start = (f32[8,512]{1,0:T(8,128)}, f32[8,512]{1,0:T(8,128)S(1)}, u32[]{:S(2)}, u32[]{:S(2)}) collective-permute-start(f32[8,512]{1,0:T(8,128)} %get-tuple-element.12.own_ref), channel_id=1, source_target_pairs={{0,128},{8,136},{16,144},{24,152},{32,160},{40,168},{48,176},{56,1... | collective-permute-start | bytes 49160 | tf_op jit(solution)/shard_map/ppermute | solution.py:380
  34.4 1.3 %collective-permute-done.near_ref = f32[8,512]{1,0:T(8,128)S(1)} collective-permute-done((f32[8,512]{1,0:T(8,128)}, f32[8,512]{1,0:T(8,128)S(1)}, u32[]{:S(2)}, u32[]{:S(2)}) %collective-permute-start) | collective-permute-done | bytes 16416 | tf_op jit(solution)/shard_map/ppermute | solution.py:380
  35.7 0.0 copy-start.1
  35.7 0.7 pad_maximum_fusion
  36.5 8.2 %collective-permute-start.1 = (f32[2,8,512]{2,1,0:T(8,128)S(1)}, f32[2,8,512]{2,1,0:T(8,128)S(1)}, u32[]{:S(2)}, u32[]{:S(2)}) collective-permute-start(f32[2,8,512]{2,1,0:T(8,128)S(1)} %pad_maximum_fusion), channel_id=1, source_target_pairs={{0,384},{8,392},{16,400},{24,408},{32,416},{40,424},{48,432},{56,4... | collective-permute-start | bytes 98312 | tf_op jit(solution)/shard_map/ppermute | solution.py:380
  44.7 1.4 %collective-permute-done.1.far_ref = f32[2,8,512]{2,1,0:T(8,128)S(1)} collective-permute-done((f32[2,8,512]{2,1,0:T(8,128)S(1)}, f32[2,8,512]{2,1,0:T(8,128)S(1)}, u32[]{:S(2)}, u32[]{:S(2)}) %collective-permute-start.1) | collective-permute-done | bytes 32800 | tf_op jit(solution)/shard_map/ppermute | solution.py:380
  46.1 0.0 copy-start.2
  46.1 0.0 copy-done.1
  46.1 0.6 copy-done.2
  46.7 1.8 %join_groups.1 = f32[384,128]{1,0:T(8,128)} custom-call(f32[8,512]{1,0:T(8,128)} %get-tuple-element.12.own_ref, f32[8,512]{1,0:T(8,128)} %copy-done.1, f32[2,8,512]{2,1,0:T(8,128)} %copy-done.2, f32[4,16,384]{2,1,0:T(8,128)} %get-tuple-element.13.state_ref, f32[4,16,128]{2,1,0:T(8,128)} %get-tuple-element.14.open_ref), custom_call_target="tpu_custom_call" | custom-call | tf_op jit(solution)/shard_map/join_groups/pallas_call | solution.py:384
  48.5 12.9 %all_to_all.20.recv_ref = f32[16,24,128]{2,1,0:T(8,128)S(1)} all-to-all(f32[16,24,128]{2,1,0:T(8,128)} %bitcast.9), channel_id=1, replica_groups={{0,8,16,24,32,40,48,56,64,72,80,88,96,104,112,120},{128,136,144,152,160..., dimensions={0} | all-to-all | bytes 393216 | tf_op jit(solution)/shard_map/all_to_all | solution.py:390
  61.3 1.8 %final_update.1 = (f32[3,64,2048]{2,1,0:T(8,128)}, f32[8,128]{1,0:T(8,128)S(1)}) custom-call(f32[16,24,128]{2,1,0:T(8,128)S(1)} %all_to_all.20.recv_ref, f32[3,64,2048]{2,1,0:T(8,128)S(1)} %get-tuple-element.15.g_ref, f32[64,128]{1,0:T(8,128)S(1)} %get-tuple-element.16.p_ref, f32[64,128]{1,0:T(8,128)S(1)} %get-tuple-element.17.q_ref), custom_call_target="tpu_custom_call" | custom-call | tf_op jit(solution)/shard_map/final_update/pallas_call | solution.py:394
  63.1 13.4 %all_to_all.21 = f32[8,1,128]{2,1,0:T(1,128)S(1)} all-to-all(f32[8,1,128]{2,1,0:T(1,128)S(1)} %bitcast.7), channel_id=1, replica_groups=mesh['gx'=64,'yz'=8] {'yz'}, dimensions={0} | all-to-all | bytes 8192 | tf_op jit(solution)/shard_map/all_to_all | solution.py:411
  76.5 0.6 reduce_sum.9
Async XLA Ops:
  1.4 1.4 %copy-start = (f32[3,64,2048]{2,1,0:T(8,128)S(1)}, f32[3,64,2048]{2,1,0:T(8,128)}, u32[]{:S(2)}) copy-start(f32[3,64,2048]{2,1,0:T(8,128)} %v_ref.1) | copy-start | bytes 4718596
  25.5 10.2 %collective-permute-start = (f32[8,512]{1,0:T(8,128)}, f32[8,512]{1,0:T(8,128)S(1)}, u32[]{:S(2)}, u32[]{:S(2)}) collective-permute-start(f32[8,512]{1,0:T(8,128)} %get-tuple-element.12.own_ref), channel_id=1, source_target_pairs={{0,128},{8,136},{16,144},{24,152},{32,160},{40,168},{48,176},{56,1... | collective-permute-start | bytes 49160 | tf_op jit(solution)/shard_map/ppermute | solution.py:380
  35.7 10.3 %copy-start.1 = (f32[8,512]{1,0:T(8,128)}, f32[8,512]{1,0:T(8,128)S(1)}, u32[]{:S(2)}) copy-start(f32[8,512]{1,0:T(8,128)S(1)} %collective-permute-done.near_ref) | copy-start | bytes 49156
  36.5 9.6 %collective-permute-start.1 = (f32[2,8,512]{2,1,0:T(8,128)S(1)}, f32[2,8,512]{2,1,0:T(8,128)S(1)}, u32[]{:S(2)}, u32[]{:S(2)}) collective-permute-start(f32[2,8,512]{2,1,0:T(8,128)S(1)} %pad_maximum_fusion), channel_id=1, source_target_pairs={{0,384},{8,392},{16,400},{24,408},{32,416},{40,424},{48,432},{56,4... | collective-permute-start | bytes 98312 | tf_op jit(solution)/shard_map/ppermute | solution.py:380
  46.1 0.6 copy-start.2

commit v2 on v1

--- a/solution.py
+++ b/solution.py
@@ -15,7 +15,11 @@
 GROUPS = 4
 LANES = 128
 CELLS = 64
+CHUNK = 512
 F32 = jnp.float32
+BF16 = jnp.bfloat16
+SMALL = pltpu.CompilerParams(vmem_limit_bytes=8 * 1024 * 1024)
+LARGE = pltpu.CompilerParams(vmem_limit_bytes=16 * 1024 * 1024)
 
 
 def lane_row(value, lanes=LANES):
@@ -26,77 +30,87 @@
     return jnp.concatenate([value] * copies, axis=1)
 
 
-def local_kernel(v_ref, block_ref, g_ref, send_ref, p_ref, q_ref, mat_ref, pad_ref, energy_ref):
-    comp = pl.program_id(0)
+def parts_of(value):
+    high = value.astype(BF16)
+    rest = value - high.astype(F32)
+    middle = rest.astype(BF16)
+    return high, middle, (rest - middle.astype(F32)).astype(BF16)
+
+
+def local_kernel(
+    v_hbm, block_hbm, g_ref, send_ref, p_ref, q_ref, v_ref, mat_ref, pad_ref, block_ref, sems
+):
+    comps, _, lines = v_ref.shape
     inner = CELLS - 2
-    lines = v_ref.shape[2]
-    row8 = lax.broadcasted_iota(jnp.int32, (8, lines), 0)
-
-    @pl.when(comp == 0)
-    def _():
-        pad_ref[...] = jnp.zeros(pad_ref.shape, F32)
-        pad_ref[0:inner, 0:inner] = block_ref[0]
-        padded = pltpu.roll(pltpu.roll(pad_ref[...], 1, 0), 1, 1)
-        first = jnp.broadcast_to(COUPLING * padded[:, 1:2], (CELLS, LANES))
-        last = jnp.broadcast_to(COUPLING * padded[:, inner : inner + 1], (CELLS, LANES))
-        p_ref[...] = first
-        q_ref[...] = last
-        cols = lax.broadcasted_iota(jnp.int32, (1, LANES), 1)
-        top = jnp.where(cols == 0, 1.0, 0.0) - COUPLING * padded[1:2]
-        bottom = jnp.where(cols == CELLS - 1, 1.0, 0.0) - COUPLING * padded[inner : inner + 1]
-        first_sum = jnp.sum(first * padded, axis=0, keepdims=True)
-        last_sum = jnp.sum(last * padded, axis=0, keepdims=True)
-        mat_ref[0:CELLS, :] = padded
-        rows = lax.broadcasted_iota(jnp.int32, (8, LANES), 0)
-        extra = jnp.where(rows == 0, top, 0.0)
-        extra = jnp.where(rows == 1, bottom, extra)
-        extra = jnp.where(rows == 2, first_sum, extra)
-        extra = jnp.where(rows == 3, last_sum, extra)
-        mat_ref[CELLS : CELLS + 8, :] = extra
-        energy_ref[...] = jnp.zeros(energy_ref.shape, F32)
-
-    v = v_ref[0]
-    low, high = v[0:1], v[CELLS - 1 : CELLS]
-    below_1 = jnp.concatenate([low, v[: CELLS - 1]], 0)
-    below_2 = jnp.concatenate([low, low, v[: CELLS - 2]], 0)
-    above_1 = jnp.concatenate([v[1:], high], 0)
-    above_2 = jnp.concatenate([v[2:], high, high], 0)
-    right = NEAR_WEIGHT * (above_1 - below_1) + FAR_WEIGHT * (above_2 - below_2)
-    out = jnp.dot(
-        mat_ref[:, 0:CELLS], right, precision=lax.Precision.HIGHEST, preferred_element_type=F32
-    )
-    g = out[0:CELLS]
-    g_ref[0] = g
-    squares = jnp.sum(g * g, axis=0, keepdims=True)
-    part = squares[:, 0:LANES]
-    for j in range(1, GROUP):
-        part = part + squares[:, j * LANES : (j + 1) * LANES]
-    energy_ref[0:1, :] += part
-    rows = out[CELLS : CELLS + 8]
-    rows = jnp.where((row8 == 4) | (row8 == 5), pltpu.roll(v[0:8], 4, 0), rows)
-    rows = jnp.where(row8 >= 6, v[CELLS - 8 : CELLS], rows)
-    at = pl.multiple_of(comp * 8, 8)
+    block_copy = pltpu.make_async_copy(block_hbm, block_ref, sems.at[comps])
+    block_copy.start()
+    copies = [pltpu.make_async_copy(v_hbm.at[c], v_ref.at[c], sems.at[c]) for c in range(comps)]
+    for copy in copies:
+        copy.start()
+
+    pad_ref[...] = jnp.zeros(pad_ref.shape, F32)
+    block_copy.wait()
+    pad_ref[0:inner, 0:inner] = block_ref[:, 0, :]
+    padded = pltpu.roll(pltpu.roll(pad_ref[...], 1, 0), 1, 1)
+    first = jnp.broadcast_to(COUPLING * padded[:, 1:2], (CELLS, LANES))
+    last = jnp.broadcast_to(COUPLING * padded[:, inner : inner + 1], (CELLS, LANES))
+    p_ref[...] = first
+    q_ref[...] = last
+    cols = lax.broadcasted_iota(jnp.int32, (1, LANES), 1)
+    top = jnp.where(cols == 0, 1.0, 0.0) - COUPLING * padded[1:2]
+    bottom = jnp.where(cols == CELLS - 1, 1.0, 0.0) - COUPLING * padded[inner : inner + 1]
+    first_sum = jnp.sum(first * padded, axis=0, keepdims=True)
+    last_sum = jnp.sum(last * padded, axis=0, keepdims=True)
+    rows = lax.broadcasted_iota(jnp.int32, (16, LANES), 0)
+    extra = jnp.where(rows == 0, top, 0.0)
+    extra = jnp.where(rows == 1, bottom, extra)
+    extra = jnp.where(rows == 2, first_sum, extra)
+    extra = jnp.where(rows == 3, last_sum, extra)
+    matrix = jnp.concatenate([padded, extra], 0)
+    high, middle, low = parts_of(matrix[:, 0:CELLS])
+    mat_ref[...] = jnp.concatenate([high, middle, low, high, middle, high], 1)
+
+    row8 = lax.broadcasted_iota(jnp.int32, (8, CHUNK), 0)
+    energy = jnp.zeros((1, LANES), F32)
+    for c in range(comps):
+        copies[c].wait()
+        for start in range(0, lines, CHUNK):
+            v = v_ref[c, :, start : start + CHUNK]
+            edge_0, edge_1 = v[0:1], v[CELLS - 1 : CELLS]
+            below_1 = jnp.concatenate([edge_0, v[: CELLS - 1]], 0)
+            below_2 = jnp.concatenate([edge_0, edge_0, v[: CELLS - 2]], 0)
+            above_1 = jnp.concatenate([v[1:], edge_1], 0)
+            above_2 = jnp.concatenate([v[2:], edge_1, edge_1], 0)
+            right = NEAR_WEIGHT * (above_1 - below_1) + FAR_WEIGHT * (above_2 - below_2)
+            high, middle, low = parts_of(right)
+            stacked = jnp.concatenate([high, high, high, middle, middle, low], 0)
+            out = jnp.dot(mat_ref[...], stacked, preferred_element_type=F32)
+            g = out[0:CELLS]
+            g_ref[c, :, start : start + CHUNK] = g
+            squares = jnp.sum(g * g, axis=0, keepdims=True)
+            rows = out[CELLS : CELLS + 8]
+            rows = jnp.where((row8 == 4) | (row8 == 5), pltpu.roll(v[0:8], 4, 0), rows)
+            rows = jnp.where(row8 >= 6, v[CELLS - 8 : CELLS], rows)
+            for j in range(CHUNK // LANES):
+                at = slice(j * LANES, (j + 1) * LANES)
+                energy = energy + squares[:, at]
+                send_ref[start // LANES + j, 8 * c : 8 * c + 8, :] = rows[:, at]
+
+    coefs = jnp.concatenate(
+        [
+            first[1:2],
+            last[1:2],
+            first[inner : inner + 1],
+            last[inner : inner + 1],
+            jnp.sum(first * first, axis=0, keepdims=True),
+            jnp.sum(first * last, axis=0, keepdims=True),
+            jnp.sum(last * last, axis=0, keepdims=True),
+            energy,
+        ],
+        0,
+    )
     for j in range(GROUP):
-        send_ref[j, pl.ds(at, 8), :] = rows[:, j * LANES : (j + 1) * LANES]
-
-    @pl.when(comp == pl.num_programs(0) - 1)
-    def _():
-        first, last = p_ref[...], q_ref[...]
-        coefs = jnp.concatenate(
-            [
-                first[1:2],
-                last[1:2],
-                first[inner : inner + 1],
-                last[inner : inner + 1],
-                jnp.sum(first * first, axis=0, keepdims=True),
-                jnp.sum(first * last, axis=0, keepdims=True),
-                jnp.sum(last * last, axis=0, keepdims=True),
-                energy_ref[0:1, :],
-            ],
-            0,
-        )
-        for j in range(GROUP):
-            send_ref[j, send_ref.shape[1] - 8 :, :] = coefs
+        send_ref[j, 8 * comps :, :] = coefs
 
 
 def group_kernel(recv_ref, msg_ref, state_ref, open_ref):
@@ -298,55 +312,59 @@
     jump_r = jnp.where(seg == GROUP - 1, right, state_ref[3])
     u = u_t - jump_l * (1.0 / 12.0)
     w = w_t - jump_r * (1.0 / 12.0)
+    stride = send_ref.shape[0] // GROUP
     send_ref[...] = jnp.zeros(send_ref.shape, F32)
     for i in range(comps):
         for r, value in enumerate((u_t, w_t, u, w)):
             part_i = value[:, i * LANES : (i + 1) * LANES]
-            send_ref[pl.ds(8 * i + r, GROUP, stride=8 * comps), :] = part_i
-    send_ref[pl.ds(4, GROUP, stride=8 * comps), :] = jnp.broadcast_to(energy, (GROUP, LANES))
-
-
-def final_kernel(recv_ref, g_ref, p_ref, q_ref, out_ref, energy_ref):
+            send_ref[pl.ds(4 * i + r, GROUP, stride=stride), :] = part_i
+    send_ref[pl.ds(4 * comps, GROUP, stride=stride), :] = jnp.broadcast_to(energy, (GROUP, LANES))
+
+
+def final_kernel(recv_ref, g_ref, p_ref, q_ref, out_hbm, energy_ref, out_ref, sems):
+    comps, _, lines = g_ref.shape
     row8 = lax.broadcasted_iota(jnp.int32, (8, LANES), 0)
     first, last = p_ref[...], q_ref[...]
-
-    @pl.when(pl.program_id(0) == 0)
-    def _():
-        energy = recv_ref[0, 4:5, :]
-        for j in range(1, GROUP):
-            energy = energy + recv_ref[j, 4:5, :]
-        energy_ref[...] = jnp.broadcast_to(energy, energy_ref.shape)
-
-    for j in range(GROUP):
-        at = slice(j * LANES, (j + 1) * LANES)
-        u_t, w_t = recv_ref[j, 0:1, :], recv_ref[j, 1:2, :]
-        u, w = recv_ref[j, 2:3, :], recv_ref[j, 3:4, :]
-        value = g_ref[0, :, at] - first * u_t - last * w_t
-        out_ref[0, 0:8, at] = jnp.where(row8 == 0, u, value[0:8])
-        out_ref[0, 8 : CELLS - 8, at] = value[8 : CELLS - 8]
-        out_ref[0, CELLS - 8 :, at] = jnp.where(row8 == 7, w, value[CELLS - 8 :])
+    energy = recv_ref[0, 4 * comps : 4 * comps + 1, :]
+    for j in range(1, GROUP):
+        energy = energy + recv_ref[j, 4 * comps : 4 * comps + 1, :]
+    energy_ref[...] = jnp.broadcast_to(energy, energy_ref.shape)
+
+    copies = []
+    for c in range(comps):
+        for j in range(GROUP):
+            at = slice(j * LANES, (j + 1) * LANES)
+            u_t, w_t, u, w = [recv_ref[j, 4 * c + r : 4 * c + r + 1, :] for r in range(4)]
+            value = g_ref[c, :, at] - first * u_t - last * w_t
+            out_ref[c, 0:8, at] = jnp.where(row8 == 0, u, value[0:8])
+            out_ref[c, 8 : CELLS - 8, at] = value[8 : CELLS - 8]
+            out_ref[c, CELLS - 8 :, at] = jnp.where(row8 == 7, w, value[CELLS - 8 :])
+        copy = pltpu.make_async_copy(out_ref.at[c], out_hbm.at[c], sems.at[c])
+        copy.start()
+        copies.append(copy)
+    for copy in copies:
+        copy.wait()
+
+
+def sum_kernel(scale, parts_ref, out_ref):
+    out_ref[0, 0] = jnp.sum(parts_ref[...]) * scale
 
 
 def on_device(velocity, blocks):
     comps, cells, lines = velocity.shape
     width = comps * LANES
+    back_rows = -(-(4 * comps + 1) // 8) * 8
     yz_count = lax.axis_size("yz")
     groups = [[GROUP * t + i for i in range(GROUP)] for t in range(GROUPS)]
     shape = functools.partial(jax.ShapeDtypeStruct, dtype=F32)
 
     g, send, p_rows, q_rows = pl.pallas_call(
         local_kernel,
-        grid=(comps,),
         in_specs=[
-            pl.BlockSpec((1, cells, lines), lambda c: (c, 0, 0)),
-            pl.BlockSpec(blocks.shape, lambda c: (0, 0, 0)),
-        ],
-        out_specs=[
-            pl.BlockSpec((1, cells, lines), lambda c: (c, 0, 0)),
-            pl.BlockSpec((GROUP, 8 * (comps + 1), LANES), lambda c: (0, 0, 0)),
-            pl.BlockSpec((cells, LANES), lambda c: (0, 0)),
-            pl.BlockSpec((cells, LANES), lambda c: (0, 0)),
-        ],
+            pl.BlockSpec(memory_space=pltpu.HBM),
+            pl.BlockSpec(memory_space=pltpu.HBM),
+        ],
+        out_specs=[pl.BlockSpec(memory_space=pltpu.VMEM)] * 4,
         out_shape=[
             shape((comps, cells, lines)),
             shape((GROUP, 8 * (comps + 1), LANES)),
@@ -354,13 +372,18 @@
             shape((cells, LANES)),
         ],
         scratch_shapes=[
-            pltpu.VMEM((cells + 8, LANES), F32),
+            pltpu.VMEM((comps, cells, lines), F32),
+            pltpu.VMEM((cells + 16, 6 * cells), BF16),
             pltpu.VMEM((cells, LANES), F32),
-            pltpu.VMEM((8, LANES), F32),
-        ],
-        compiler_params=pltpu.CompilerParams(vmem_limit_bytes=32 * 1024 * 1024),
+            pltpu.VMEM((cells - 2, 1, cells - 2), F32),
+            pltpu.SemaphoreType.DMA((comps + 1,)),
+        ],
+        compiler_params=LARGE,
         name="local_solve",
-    )(velocity, blocks)
+    )(
+        pltpu.with_memory_space_constraint(velocity, pltpu.HBM),
+        pltpu.with_memory_space_constraint(jnp.transpose(blocks, (1, 0, 2)), pltpu.HBM),
+    )
 
     recv = lax.all_to_all(send, "gx", 0, 0, axis_index_groups=groups, tiled=True)
     msg, state, opened = pl.pallas_call(
@@ -370,6 +393,7 @@
             shape((4, GROUP, width)),
             shape((4, GROUP, LANES)),
         ],
+        compiler_params=SMALL,
         name="group_solve",
     )(recv.reshape(GROUP * 8 * (comps + 1), LANES))
 
@@ -383,34 +407,40 @@
     far = swapped(jnp.stack([msg, near]), 3)
     send_back = pl.pallas_call(
         join_kernel,
-        out_shape=shape((GROUP * 8 * comps, LANES)),
+        out_shape=shape((GROUP * back_rows, LANES)),
         scratch_shapes=[pltpu.VMEM((GROUPS, 8, width + LANES), F32)],
+        compiler_params=SMALL,
         name="join_groups",
     )(msg, near, far, state, opened)
     back = lax.all_to_all(
-        send_back.reshape(GROUP, 8 * comps, LANES), "gx", 0, 0, axis_index_groups=groups, tiled=True
+        send_back.reshape(GROUP, back_rows, LANES), "gx", 0, 0, axis_index_groups=groups, tiled=True
     )
 
     derivative, energy = pl.pallas_call(
         final_kernel,
-        grid=(comps,),
-        in_specs=[
-            pl.BlockSpec((GROUP, 8, LANES), lambda c: (0, c, 0)),
-            pl.BlockSpec((1, cells, lines), lambda c: (c, 0, 0)),
-            pl.BlockSpec((cells, LANES), lambda c: (0, 0)),
-            pl.BlockSpec((cells, LANES), lambda c: (0, 0)),
-        ],
+        in_specs=[pl.BlockSpec(memory_space=pltpu.VMEM)] * 4,
         out_specs=[
-            pl.BlockSpec((1, cells, lines), lambda c: (c, 0, 0)),
-            pl.BlockSpec((yz_count, LANES), lambda c: (0, 0)),
+            pl.BlockSpec(memory_space=pltpu.HBM),
+            pl.BlockSpec(memory_space=pltpu.VMEM),
         ],
         out_shape=[shape((comps, cells, lines)), shape((yz_count, LANES))],
-        compiler_params=pltpu.CompilerParams(vmem_limit_bytes=32 * 1024 * 1024),
+        scratch_shapes=[
+            pltpu.VMEM((comps, cells, lines), F32),
+            pltpu.SemaphoreType.DMA((comps,)),
+        ],
+        compiler_params=LARGE,
         name="final_update",
     )(back, g, p_rows, q_rows)
     energies = lax.all_to_all(energy, "yz", 0, 0, tiled=True)
     total_count = comps * cells * lines * lax.axis_size("gx") * yz_count
-    return derivative, jnp.sum(energies) / total_count
+    mean_square = pl.pallas_call(
+        functools.partial(sum_kernel, 1.0 / total_count),
+        out_specs=pl.BlockSpec(memory_space=pltpu.SMEM),
+        out_shape=shape((1, 1)),
+        compiler_params=SMALL,
+        name="mean_square",
+    )(energies)
+    return derivative, mean_square[0, 0]
 
 
 def solution(mesh):

time: 79.5 us -> 69.6 us (0.88)
  local copies, waits for them, and re-layouts: 2.77 us -> 0 us
  Pallas kernels: 7.81 us -> 5.26 us
  between operations: 2.44 us -> 0.67 us
  other arithmetic: 1.34 us -> 0.01 us
  blocking collectives: 44.7 us -> 43.9 us
    unnamed x7 -> x0, local copies, waits for them, and re-layouts: 2.77 us -> none
    pallas_call x1, Pallas kernels: 1.87 us -> 0.33 us  [on_device(): pl.pallas_call(group_kernel, out_shape=[shape((8, width + LANES)), shape(...]
    pallas_call x3 -> x4, Pallas kernels: 5.94 us -> 4.93 us  [the longest x1 2.83 us: on_device(): pl.pallas_call(local_kernel, in_specs=[pl.BlockSpec(memory_space=pltpu.HB...]
where the time goes in v2:
time: 69.6 us; the launch traced here: 69.3 us
  blocking collectives  43.9 us (63%)
  starting transfers between devices  17 us (24%)
  Pallas kernels  5.26 us (8%)
  waiting for transfers between devices  2.48 us (4%)
    all_to_all x1, blocking collectives, on_device(): lax.all_to_all(send, 'gx', 0, 0, axis_index_groups=groups, tiled=True)  18.5 us
    ppermute x2, starting transfers between devices, swapped(): return lax.ppermute(value, 'gx', pairs)  17 us
    all_to_all x1, blocking collectives, on_device(): energies = lax.all_to_all(energy, 'yz', 0, 0, tiled=True)  13.2 us
    all_to_all x1, blocking collectives, on_device(): lax.all_to_all(send_back.reshape(GROUP, back_rows, LANES), 'gx', 0, 0, ax...  12.2 us
    pallas_call x1, Pallas kernels, on_device(): pl.pallas_call(local_kernel, in_specs=[pl.BlockSpec(memory_space=pltpu.HB...  2.83 us
    ppermute x2, waiting for transfers between devices, swapped(): return lax.ppermute(value, 'gx', pairs)  2.48 us
  transfers between devices with their start and end apart: 2, of which 2 were waited for; matrix products, arithmetic and copies ran while one was open for 0% of the time, Pallas kernels for 0%

profile of v2, /device:TPU:1, one launch (start us, length us, event | category | flops | bytes accessed | tf_op | source)
XLA Modules:
  0.0 69.3 jit_solution(7218415201712056434)
XLA Ops:
  0.6 2.8 %local_solve.1 = (f32[3,64,2048]{2,1,0:T(8,128)S(1)}, f32[16,32,128]{2,1,0:T(8,128)S(1)}, f32[64,128]{1,0:T(8,128)S(1)}, f32[64,128]{1,0:T(8,128)S(1)}) custom-call(f32[3,64,2048]{2,1,0:T(8,128)} %v_hbm.1, f32[62,1,62]{2,1,0:T(1,128)} %bitcast.16), custom_call_target="tpu_custom_call" | custom-call | tf_op jit(solution)/shard_map/local_solve/pallas_call | solution.py:361
  3.5 18.5 %all_to_all.21 = f32[16,32,128]{2,1,0:T(8,128)S(1)} all-to-all(f32[16,32,128]{2,1,0:T(8,128)S(1)} %get-tuple-element.11), channel_id=1, replica_groups={{0,8,16,24,32,40,48,56,64,72,80,88,96,104,112,120},{128,136,144,152,160..., dimensions={0} | all-to-all | bytes 524288 | tf_op jit(solution)/shard_map/all_to_all | solution.py:388
  22.0 0.3 group_solve.1
  22.3 8.8 %collective-permute-start = (f32[8,512]{1,0:T(8,128)S(1)}, f32[8,512]{1,0:T(8,128)S(1)}, u32[]{:S(2)}, u32[]{:S(2)}) collective-permute-start(f32[8,512]{1,0:T(8,128)S(1)} %get-tuple-element.12.own_ref), channel_id=1, source_target_pairs={{0,128},{8,136},{16,144},{24,152},{32,160},{40,168},{48,176},{56,1... | collective-permute-start | bytes 49160 | tf_op jit(solution)/shard_map/ppermute | solution.py:404
  31.1 1.1 %collective-permute-done.near_ref = f32[8,512]{1,0:T(8,128)S(1)} collective-permute-done((f32[8,512]{1,0:T(8,128)S(1)}, f32[8,512]{1,0:T(8,128)S(1)}, u32[]{:S(2)}, u32[]{:S(2)}) %collective-permute-start) | collective-permute-done | bytes 16416 | tf_op jit(solution)/shard_map/ppermute | solution.py:404
  32.2 8.2 %collective-permute-start.1 = (f32[2,8,512]{2,1,0:T(8,128)S(1)}, f32[2,8,512]{2,1,0:T(8,128)S(1)}, u32[]{:S(2)}, u32[]{:S(2)}) collective-permute-start(f32[2,8,512]{2,1,0:T(8,128)S(1)} %pad_maximum_fusion), channel_id=1, source_target_pairs={{0,384},{8,392},{16,400},{24,408},{32,416},{40,424},{48,432},{56,4... | collective-permute-start | bytes 98312 | tf_op jit(solution)/shard_map/ppermute | solution.py:404
  40.4 1.4 %collective-permute-done.1.far_ref = f32[2,8,512]{2,1,0:T(8,128)S(1)} collective-permute-done((f32[2,8,512]{2,1,0:T(8,128)S(1)}, f32[2,8,512]{2,1,0:T(8,128)S(1)}, u32[]{:S(2)}, u32[]{:S(2)}) %collective-permute-start.1) | collective-permute-done | bytes 32800 | tf_op jit(solution)/shard_map/ppermute | solution.py:404
  41.8 0.2 join_groups.1
  42.0 12.2 %all_to_all.22.recv_ref = f32[16,16,128]{2,1,0:T(8,128)S(1)} all-to-all(f32[16,16,128]{2,1,0:T(8,128)S(1)} %bitcast.11), channel_id=1, replica_groups={{0,8,16,24,32,40,48,56,64,72,80,88,96,104,112,120},{128,136,144,152,160..., dimensions={0} | all-to-all | bytes 262144 | tf_op jit(solution)/shard_map/all_to_all | solution.py:415
  54.2 1.2 %final_update.1 = (f32[3,64,2048]{2,1,0:T(8,128)}, f32[8,128]{1,0:T(8,128)S(1)}) custom-call(f32[16,16,128]{2,1,0:T(8,128)S(1)} %all_to_all.22.recv_ref, f32[3,64,2048]{2,1,0:T(8,128)S(1)} %get-tuple-element.15.g_ref, f32[64,128]{1,0:T(8,128)S(1)} %get-tuple-element.16.p_ref, f32[64,128]{1,0:T(8,128)S(1)} %get-tuple-element.17.q_ref), custom_call_target="tpu_custom_call" | custom-call | tf_op jit(solution)/shard_map/final_update/pallas_call | solution.py:419
  55.5 13.2 %all_to_all.23 = f32[8,1,128]{2,1,0:T(1,128)S(1)} all-to-all(f32[8,1,128]{2,1,0:T(1,128)S(1)} %bitcast.15), channel_id=1, replica_groups=mesh['gx'=64,'yz'=8] {'yz'}, dimensions={0} | all-to-all | bytes 8192 | tf_op jit(solution)/shard_map/all_to_all | solution.py:434
  68.7 0.6 mean_square.1
  (1 shorter events, 0.0 us)
Async XLA Ops:
  22.3 9.9 %collective-permute-start = (f32[8,512]{1,0:T(8,128)S(1)}, f32[8,512]{1,0:T(8,128)S(1)}, u32[]{:S(2)}, u32[]{:S(2)}) collective-permute-start(f32[8,512]{1,0:T(8,128)S(1)} %get-tuple-element.12.own_ref), channel_id=1, source_target_pairs={{0,128},{8,136},{16,144},{24,152},{32,160},{40,168},{48,176},{56,1... | collective-permute-start | bytes 49160 | tf_op jit(solution)/shard_map/ppermute | solution.py:404
  32.2 9.6 %collective-permute-start.1 = (f32[2,8,512]{2,1,0:T(8,128)S(1)}, f32[2,8,512]{2,1,0:T(8,128)S(1)}, u32[]{:S(2)}, u32[]{:S(2)}) collective-permute-start(f32[2,8,512]{2,1,0:T(8,128)S(1)} %pad_maximum_fusion), channel_id=1, source_target_pairs={{0,384},{8,392},{16,400},{24,408},{32,416},{40,424},{48,432},{56,4... | collective-permute-start | bytes 98312 | tf_op jit(solution)/shard_map/ppermute | solution.py:404

commit v3 on v2

--- a/solution.py
+++ b/solution.py
@@ -38,18 +38,61 @@
 
 
 def local_kernel(
-    v_hbm, block_hbm, g_ref, send_ref, p_ref, q_ref, v_ref, mat_ref, pad_ref, block_ref, sems
+    v_hbm, block_hbm, g_ref, send_ref, p_ref, q_ref, v_ref, mat_ref, pad_ref, block_ref, part_ref, sems
 ):
     comps, _, lines = v_ref.shape
     inner = CELLS - 2
+    stride = send_ref.shape[0] // GROUP
+    copies = [pltpu.make_async_copy(v_hbm.at[c], v_ref.at[c], sems.at[c]) for c in range(comps)]
     block_copy = pltpu.make_async_copy(block_hbm, block_ref, sems.at[comps])
+    copies[0].start()
     block_copy.start()
-    copies = [pltpu.make_async_copy(v_hbm.at[c], v_ref.at[c], sems.at[c]) for c in range(comps)]
-    for copy in copies:
+    for copy in copies[1:]:
         copy.start()
 
+    def split_right(c):
+        for start in range(0, lines, CHUNK):
+            at = slice(start, start + CHUNK)
+            v = v_ref[c, :, at]
+            edge_0, edge_1 = v[0:1], v[CELLS - 1 : CELLS]
+            below_1 = jnp.concatenate([edge_0, v[: CELLS - 1]], 0)
+            below_2 = jnp.concatenate([edge_0, edge_0, v[: CELLS - 2]], 0)
+            above_1 = jnp.concatenate([v[1:], edge_1], 0)
+            above_2 = jnp.concatenate([v[2:], edge_1, edge_1], 0)
+            right = NEAR_WEIGHT * (above_1 - below_1) + FAR_WEIGHT * (above_2 - below_2)
+            for i, part in enumerate(parts_of(right)):
+                part_ref[c, i * CELLS : (i + 1) * CELLS, at] = part
+
+    row8 = lax.broadcasted_iota(jnp.int32, (8, CHUNK), 0)
+
+    def multiply(c, squares):
+        for start in range(0, lines, CHUNK):
+            at = slice(start, start + CHUNK)
+            high = part_ref[c, 0:CELLS, at]
+            middle = part_ref[c, CELLS : 2 * CELLS, at]
+            low = part_ref[c, 2 * CELLS : 3 * CELLS, at]
+            stacked = jnp.concatenate([high, high, high, middle, middle, low], 0)
+            out = jnp.dot(mat_ref[...], stacked, preferred_element_type=F32)
+            g = out[0:CELLS]
+            g_ref[c, :, at] = g
+            square = g * g
+            tiles = [square[8 * i : 8 * i + 8] for i in range(CELLS // 8)]
+            while len(tiles) > 1:
+                tiles = [x + y for x, y in zip(tiles[0::2], tiles[1::2])]
+            squares = squares + tiles[0]
+            rows = out[CELLS : CELLS + 8]
+            rows = jnp.where((row8 == 4) | (row8 == 5), pltpu.roll(v_ref[c, 0:8, at], 4, 0), rows)
+            rows = jnp.where(row8 >= 6, v_ref[c, CELLS - 8 : CELLS, at], rows)
+            for j in range(CHUNK // LANES):
+                to = stride * (start // LANES + j) + 8 * c
+                send_ref[to : to + 8, :] = rows[:, j * LANES : (j + 1) * LANES]
+        return squares
+
+    copies[0].wait()
+    split_right(0)
+    copies[1].wait()
+    block_copy.wait()
     pad_ref[...] = jnp.zeros(pad_ref.shape, F32)
-    block_copy.wait()
     pad_ref[0:inner, 0:inner] = block_ref[:, 0, :]
     padded = pltpu.roll(pltpu.roll(pad_ref[...], 1, 0), 1, 1)
     first = jnp.broadcast_to(COUPLING * padded[:, 1:2], (CELLS, LANES))
@@ -69,61 +112,48 @@
     matrix = jnp.concatenate([padded, extra], 0)
     high, middle, low = parts_of(matrix[:, 0:CELLS])
     mat_ref[...] = jnp.concatenate([high, middle, low, high, middle, high], 1)
-
-    row8 = lax.broadcasted_iota(jnp.int32, (8, CHUNK), 0)
-    energy = jnp.zeros((1, LANES), F32)
-    for c in range(comps):
+    split_right(1)
+    squares = multiply(0, jnp.zeros((8, CHUNK), F32))
+    for c in range(2, comps):
         copies[c].wait()
-        for start in range(0, lines, CHUNK):
-            v = v_ref[c, :, start : start + CHUNK]
-            edge_0, edge_1 = v[0:1], v[CELLS - 1 : CELLS]
-            below_1 = jnp.concatenate([edge_0, v[: CELLS - 1]], 0)
-            below_2 = jnp.concatenate([edge_0, edge_0, v[: CELLS - 2]], 0)
-            above_1 = jnp.concatenate([v[1:], edge_1], 0)
-            above_2 = jnp.concatenate([v[2:], edge_1, edge_1], 0)
-            right = NEAR_WEIGHT * (above_1 - below_1) + FAR_WEIGHT * (above_2 - below_2)
-            high, middle, low = parts_of(right)
-            stacked = jnp.concatenate([high, high, high, middle, middle, low], 0)
-            out = jnp.dot(mat_ref[...], stacked, preferred_element_type=F32)
-            g = out[0:CELLS]
-            g_ref[c, :, start : start + CHUNK] = g
-            squares = jnp.sum(g * g, axis=0, keepdims=True)
-            rows = out[CELLS : CELLS + 8]
-            rows = jnp.where((row8 == 4) | (row8 == 5), pltpu.roll(v[0:8], 4, 0), rows)
-            rows = jnp.where(row8 >= 6, v[CELLS - 8 : CELLS], rows)
-            for j in range(CHUNK // LANES):
-                at = slice(j * LANES, (j + 1) * LANES)
-                energy = energy + squares[:, at]
-                send_ref[start // LANES + j, 8 * c : 8 * c + 8, :] = rows[:, at]
-
-    coefs = jnp.concatenate(
-        [
-            first[1:2],
-            last[1:2],
-            first[inner : inner + 1],
-            last[inner : inner + 1],
-            jnp.sum(first * first, axis=0, keepdims=True),
-            jnp.sum(first * last, axis=0, keepdims=True),
-            jnp.sum(last * last, axis=0, keepdims=True),
-            energy,
-        ],
-        0,
-    )
+        split_right(c)
+        squares = multiply(c - 1, squares)
+    squares = multiply(comps - 1, squares)
+
+    energy = squares[:, 0:LANES]
+    for j in range(1, CHUNK // LANES):
+        energy = energy + squares[:, j * LANES : (j + 1) * LANES]
+    energy = jnp.sum(energy, axis=0, keepdims=True)
+    coefs = energy + pltpu.roll(energy, LANES // 2, 1)
+    numbers = [
+        first[1:2],
+        last[1:2],
+        first[inner : inner + 1],
+        last[inner : inner + 1],
+        jnp.sum(first * first, axis=0, keepdims=True),
+        jnp.sum(first * last, axis=0, keepdims=True),
+        jnp.sum(last * last, axis=0, keepdims=True),
+    ]
+    for i, number in enumerate(numbers):
+        coefs = jnp.where(cols == i, number, coefs)
     for j in range(GROUP):
-        send_ref[j, 8 * comps :, :] = coefs
+        to = stride * j + 8 * comps
+        send_ref[to : to + 1, :] = coefs
 
 
 def group_kernel(recv_ref, msg_ref, state_ref, open_ref):
     stride = recv_ref.shape[0] // GROUP
-    comps = stride // 8 - 1
+    comps = stride // 8
     width = comps * LANES
 
     def rows(r):
         parts = [recv_ref[pl.ds(8 * i + r, GROUP, stride=stride), :] for i in range(comps)]
         return jnp.concatenate(parts, 1)
 
+    numbers = recv_ref[pl.ds(8 * comps, GROUP, stride=stride), :]
+
     def coef(r):
-        return recv_ref[pl.ds(8 * comps + r, GROUP, stride=stride), :]
+        return jnp.broadcast_to(numbers[:, r : r + 1], (GROUP, LANES))
 
     seg = lax.broadcasted_iota(jnp.int32, (GROUP, width), 0)
     seg_1 = lax.broadcasted_iota(jnp.int32, (GROUP, LANES), 0)
@@ -135,7 +165,9 @@
         return pltpu.roll(x, GROUP - s, 0)
 
     b_first, b_last, pg, qg, v_0, v_1, v_62, v_63 = [rows(r) for r in range(8)]
-    p_0, q_0, p_61, q_61, pp, pq, qq, energy = [coef(r) for r in range(8)]
+    p_0, q_0, p_61, q_61, pp, pq, qq = [coef(r) for r in range(7)]
+    upper = lax.broadcasted_iota(jnp.int32, (GROUP, LANES), 1) >= LANES // 2
+    energy = jnp.where(upper, numbers, 0.0)
     jump_l = jnp.where(seg == 0, 0.0, prev(v_63) - v_0)
     jump_l2 = jnp.where(seg == 0, 0.0, prev(v_62) - v_0)
     jump_r = jnp.where(seg == GROUP - 1, 0.0, v_63 - following(v_0))
@@ -313,7 +345,6 @@
     u = u_t - jump_l * (1.0 / 12.0)
     w = w_t - jump_r * (1.0 / 12.0)
     stride = send_ref.shape[0] // GROUP
-    send_ref[...] = jnp.zeros(send_ref.shape, F32)
     for i in range(comps):
         for r, value in enumerate((u_t, w_t, u, w)):
             part_i = value[:, i * LANES : (i + 1) * LANES]
@@ -321,20 +352,23 @@
     send_ref[pl.ds(4 * comps, GROUP, stride=stride), :] = jnp.broadcast_to(energy, (GROUP, LANES))
 
 
-def final_kernel(recv_ref, g_ref, p_ref, q_ref, out_hbm, energy_ref, out_ref, sems):
+def energy_kernel(recv_ref, out_ref):
+    stride = recv_ref.shape[0] // GROUP
+    energy = recv_ref[pl.ds(stride - 1, GROUP, stride=stride), :]
+    out_ref[...] = jnp.broadcast_to(jnp.sum(energy, axis=0, keepdims=True), out_ref.shape)
+
+
+def final_kernel(scale, recv_ref, energy_ref, g_ref, p_ref, q_ref, out_hbm, mean_ref, out_ref, sems):
     comps, _, lines = g_ref.shape
+    stride = recv_ref.shape[0] // GROUP
     row8 = lax.broadcasted_iota(jnp.int32, (8, LANES), 0)
     first, last = p_ref[...], q_ref[...]
-    energy = recv_ref[0, 4 * comps : 4 * comps + 1, :]
-    for j in range(1, GROUP):
-        energy = energy + recv_ref[j, 4 * comps : 4 * comps + 1, :]
-    energy_ref[...] = jnp.broadcast_to(energy, energy_ref.shape)
-
     copies = []
     for c in range(comps):
         for j in range(GROUP):
             at = slice(j * LANES, (j + 1) * LANES)
-            u_t, w_t, u, w = [recv_ref[j, 4 * c + r : 4 * c + r + 1, :] for r in range(4)]
+            base = stride * j + 4 * c
+            u_t, w_t, u, w = [recv_ref[base + r : base + r + 1, :] for r in range(4)]
             value = g_ref[c, :, at] - first * u_t - last * w_t
             out_ref[c, 0:8, at] = jnp.where(row8 == 0, u, value[0:8])
             out_ref[c, 8 : CELLS - 8, at] = value[8 : CELLS - 8]
@@ -342,18 +376,15 @@
         copy = pltpu.make_async_copy(out_ref.at[c], out_hbm.at[c], sems.at[c])
         copy.start()
         copies.append(copy)
+    mean_ref[0, 0] = jnp.sum(energy_ref[...]) * scale
     for copy in copies:
         copy.wait()
-
-
-def sum_kernel(scale, parts_ref, out_ref):
-    out_ref[0, 0] = jnp.sum(parts_ref[...]) * scale
 
 
 def on_device(velocity, blocks):
     comps, cells, lines = velocity.shape
     width = comps * LANES
-    back_rows = -(-(4 * comps + 1) // 8) * 8
+    send_rows, back_rows = 8 * comps + 1, 4 * comps + 1
     yz_count = lax.axis_size("yz")
     groups = [[GROUP * t + i for i in range(GROUP)] for t in range(GROUPS)]
     shape = functools.partial(jax.ShapeDtypeStruct, dtype=F32)
@@ -367,7 +398,7 @@
         out_specs=[pl.BlockSpec(memory_space=pltpu.VMEM)] * 4,
         out_shape=[
             shape((comps, cells, lines)),
-            shape((GROUP, 8 * (comps + 1), LANES)),
+            shape((GROUP * send_rows, LANES)),
             shape((cells, LANES)),
             shape((cells, LANES)),
         ],
@@ -376,6 +407,7 @@
             pltpu.VMEM((cells + 16, 6 * cells), BF16),
             pltpu.VMEM((cells, LANES), F32),
             pltpu.VMEM((cells - 2, 1, cells - 2), F32),
+            pltpu.VMEM((comps, 3 * cells, lines), BF16),
             pltpu.SemaphoreType.DMA((comps + 1,)),
         ],
         compiler_params=LARGE,
@@ -385,7 +417,11 @@
         pltpu.with_memory_space_constraint(jnp.transpose(blocks, (1, 0, 2)), pltpu.HBM),
     )
 
-    recv = lax.all_to_all(send, "gx", 0, 0, axis_index_groups=groups, tiled=True)
+    def spread(value, axis, **kwargs):
+        rows = value.reshape(value.shape[0], 1, LANES)
+        return lax.all_to_all(rows, axis, 0, 0, tiled=True, **kwargs).reshape(value.shape)
+
+    recv = spread(send, "gx", axis_index_groups=groups)
     msg, state, opened = pl.pallas_call(
         group_kernel,
         out_shape=[
@@ -395,7 +431,7 @@
         ],
         compiler_params=SMALL,
         name="group_solve",
-    )(recv.reshape(GROUP * 8 * (comps + 1), LANES))
+    )(recv)
 
     def swapped(value, mask):
         pairs = [
@@ -412,34 +448,30 @@
         compiler_params=SMALL,
         name="join_groups",
     )(msg, near, far, state, opened)
-    back = lax.all_to_all(
-        send_back.reshape(GROUP, back_rows, LANES), "gx", 0, 0, axis_index_groups=groups, tiled=True
-    )
-
-    derivative, energy = pl.pallas_call(
-        final_kernel,
-        in_specs=[pl.BlockSpec(memory_space=pltpu.VMEM)] * 4,
+    back = spread(send_back, "gx", axis_index_groups=groups)
+    energy = pl.pallas_call(
+        energy_kernel,
+        out_shape=shape((yz_count, LANES)),
+        compiler_params=SMALL,
+        name="line_energy",
+    )(back)
+    energies = spread(energy, "yz")
+    total_count = comps * cells * lines * lax.axis_size("gx") * yz_count
+    derivative, mean_square = pl.pallas_call(
+        functools.partial(final_kernel, 1.0 / total_count),
+        in_specs=[pl.BlockSpec(memory_space=pltpu.VMEM)] * 5,
         out_specs=[
             pl.BlockSpec(memory_space=pltpu.HBM),
-            pl.BlockSpec(memory_space=pltpu.VMEM),
-        ],
-        out_shape=[shape((comps, cells, lines)), shape((yz_count, LANES))],
+            pl.BlockSpec(memory_space=pltpu.SMEM),
+        ],
+        out_shape=[shape((comps, cells, lines)), shape((1, 1))],
         scratch_shapes=[
             pltpu.VMEM((comps, cells, lines), F32),
             pltpu.SemaphoreType.DMA((comps,)),
         ],
         compiler_params=LARGE,
         name="final_update",
-    )(back, g, p_rows, q_rows)
-    energies = lax.all_to_all(energy, "yz", 0, 0, tiled=True)
-    total_count = comps * cells * lines * lax.axis_size("gx") * yz_count
-    mean_square = pl.pallas_call(
-        functools.partial(sum_kernel, 1.0 / total_count),
-        out_specs=pl.BlockSpec(memory_space=pltpu.SMEM),
-        out_shape=shape((1, 1)),
-        compiler_params=SMALL,
-        name="mean_square",
-    )(energies)
+    )(back, energies, g, p_rows, q_rows)
     return derivative, mean_square[0, 0]
 
 

time: 69.6 us -> 68.6 us (0.986)
  blocking collectives: 43.9 us -> 42.6 us
    all_to_all x3, blocking collectives: 43.9 us -> 42.6 us  [spread(): lax.all_to_all(rows, axis, 0, 0, tiled=True, **kwargs).reshape(value.shape)]
where the time goes in v3:
time: 68.6 us; the launch traced here: 68.3 us
  blocking collectives  42.6 us (62%)
  starting transfers between devices  17 us (25%)
  Pallas kernels  5.57 us (8%)
  waiting for transfers between devices  2.4 us (3%)
    all_to_all x3, blocking collectives, spread(): lax.all_to_all(rows, axis, 0, 0, tiled=True, **kwargs).reshape(value.shape)  42.6 us
    ppermute x2, starting transfers between devices, swapped(): return lax.ppermute(value, 'gx', pairs)  17 us
    pallas_call x1, Pallas kernels, on_device(): pl.pallas_call(local_kernel, in_specs=[pl.BlockSpec(memory_space=pltpu.HB...  3.32 us
    ppermute x2, waiting for transfers between devices, swapped(): return lax.ppermute(value, 'gx', pairs)  2.4 us
    pallas_call x1, Pallas kernels, on_device(): pl.pallas_call(functools.partial(final_kernel, 1.0 / total_count), in_spe...  1.78 us
  transfers between devices with their start and end apart: 2, of which 2 were waited for; matrix products, arithmetic and copies ran while one was open for 0% of the time, Pallas kernels for 0%

profile of v3, /device:TPU:1, one launch (start us, length us, event | category | flops | bytes accessed | tf_op | source)
XLA Modules:
  0.0 68.3 jit_solution(1404104451069771234)
XLA Ops:
  0.6 3.3 %local_solve.1 = (f32[3,64,2048]{2,1,0:T(8,128)S(1)}, f32[400,128]{1,0:T(8,128)S(1)}, f32[64,128]{1,0:T(8,128)S(1)}, f32[64,128]{1,0:T(8,128)S(1)}) custom-call(f32[3,64,2048]{2,1,0:T(8,128)} %v_hbm.1, f32[62,1,62]{2,1,0:T(1,128)} %bitcast.25), custom_call_target="tpu_custom_call" | custom-call | tf_op jit(solution)/shard_map/local_solve/pallas_call | solution.py:392
  4.0 17.5 %all_to_all.15 = f32[400,1,128]{2,1,0:T(1,128)S(1)} all-to-all(f32[400,1,128]{2,1,0:T(1,128)S(1)} %bitcast.20), channel_id=1, replica_groups={{0,8,16,24,32,40,48,56,64,72,80,88,96,104,112,120},{128,136,144,152,160..., dimensions={0} | all-to-all | bytes 409600 | tf_op jit(solution)/shard_map/all_to_all | solution.py:422
  21.5 0.3 group_solve.1
  21.8 8.8 %collective-permute-start = (f32[8,512]{1,0:T(8,128)S(1)}, f32[8,512]{1,0:T(8,128)S(1)}, u32[]{:S(2)}, u32[]{:S(2)}) collective-permute-start(f32[8,512]{1,0:T(8,128)S(1)} %get-tuple-element.12.own_ref), channel_id=1, source_target_pairs={{0,128},{8,136},{16,144},{24,152},{32,160},{40,168},{48,176},{56,1... | collective-permute-start | bytes 49160 | tf_op jit(solution)/shard_map/ppermute | solution.py:440
  30.6 1.1 %collective-permute-done.near_ref = f32[8,512]{1,0:T(8,128)S(1)} collective-permute-done((f32[8,512]{1,0:T(8,128)S(1)}, f32[8,512]{1,0:T(8,128)S(1)}, u32[]{:S(2)}, u32[]{:S(2)}) %collective-permute-start) | collective-permute-done | bytes 16416 | tf_op jit(solution)/shard_map/ppermute | solution.py:440
  31.7 8.2 %collective-permute-start.1 = (f32[2,8,512]{2,1,0:T(8,128)S(1)}, f32[2,8,512]{2,1,0:T(8,128)S(1)}, u32[]{:S(2)}, u32[]{:S(2)}) collective-permute-start(f32[2,8,512]{2,1,0:T(8,128)S(1)} %pad_maximum_fusion), channel_id=1, source_target_pairs={{0,384},{8,392},{16,400},{24,408},{32,416},{40,424},{48,432},{56,4... | collective-permute-start | bytes 98312 | tf_op jit(solution)/shard_map/ppermute | solution.py:440
  39.9 1.3 %collective-permute-done.1.far_ref = f32[2,8,512]{2,1,0:T(8,128)S(1)} collective-permute-done((f32[2,8,512]{2,1,0:T(8,128)S(1)}, f32[2,8,512]{2,1,0:T(8,128)S(1)}, u32[]{:S(2)}, u32[]{:S(2)}) %collective-permute-start.1) | collective-permute-done | bytes 32800 | tf_op jit(solution)/shard_map/ppermute | solution.py:440
  41.2 0.2 join_groups.1
  41.4 12.2 %all_to_all.16 = f32[208,1,128]{2,1,0:T(1,128)S(1)} all-to-all(f32[208,1,128]{2,1,0:T(1,128)S(1)} %bitcast.19), channel_id=1, replica_groups={{0,8,16,24,32,40,48,56,64,72,80,88,96,104,112,120},{128,136,144,152,160..., dimensions={0} | all-to-all | bytes 212992 | tf_op jit(solution)/shard_map/all_to_all | solution.py:422
  53.6 12.9 %all_to_all.17 = f32[8,1,128]{2,1,0:T(1,128)S(1)} all-to-all(f32[8,1,128]{2,1,0:T(1,128)S(1)} %bitcast.24), channel_id=1, replica_groups=mesh['gx'=64,'yz'=8] {'yz'}, dimensions={0} | all-to-all | bytes 8192 | tf_op jit(solution)/shard_map/all_to_all | solution.py:422
  66.5 1.8 %final_update.1 = (f32[3,64,2048]{2,1,0:T(8,128)}, f32[1,1]{1,0:T(1,128)}) custom-call(f32[208,128]{1,0:T(8,128)S(1)} %bitcast.17, f32[8,128]{1,0:T(8,128)S(1)} %bitcast.23, f32[3,64,2048]{2,1,0:T(8,128)S(1)} %get-tuple-element.15.g_ref, f32[64,128]{1,0:T(8,128)S(1)} %get-tuple-element.16.p_ref, f32[64,128]{1,0:T(8,128)S(1)} %get-tuple-element.17.q_ref), custom_call_target="tpu_custom_call" | custom-call | tf_op jit(solution)/shard_map/final_update/pallas_call | solution.py:460
  (2 shorter events, 0.0 us)
Async XLA Ops:
  21.8 9.9 %collective-permute-start = (f32[8,512]{1,0:T(8,128)S(1)}, f32[8,512]{1,0:T(8,128)S(1)}, u32[]{:S(2)}, u32[]{:S(2)}) collective-permute-start(f32[8,512]{1,0:T(8,128)S(1)} %get-tuple-element.12.own_ref), channel_id=1, source_target_pairs={{0,128},{8,136},{16,144},{24,152},{32,160},{40,168},{48,176},{56,1... | collective-permute-start | bytes 49160 | tf_op jit(solution)/shard_map/ppermute | solution.py:440
  31.7 9.5 %collective-permute-start.1 = (f32[2,8,512]{2,1,0:T(8,128)S(1)}, f32[2,8,512]{2,1,0:T(8,128)S(1)}, u32[]{:S(2)}, u32[]{:S(2)}) collective-permute-start(f32[2,8,512]{2,1,0:T(8,128)S(1)} %pad_maximum_fusion), channel_id=1, source_target_pairs={{0,384},{8,392},{16,400},{24,408},{32,416},{40,424},{48,432},{56,4... | collective-permute-start | bytes 98312 | tf_op jit(solution)/shard_map/ppermute | solution.py:440

commit v4 on v3

--- a/solution.py
+++ b/solution.py
@@ -38,61 +38,19 @@
 
 
 def local_kernel(
-    v_hbm, block_hbm, g_ref, send_ref, p_ref, q_ref, v_ref, mat_ref, pad_ref, block_ref, part_ref, sems
+    v_hbm, block_hbm, g_ref, send_ref, p_ref, q_ref, v_ref, mat_ref, pad_ref, block_ref, sems
 ):
     comps, _, lines = v_ref.shape
     inner = CELLS - 2
     stride = send_ref.shape[0] // GROUP
+    block_copy = pltpu.make_async_copy(block_hbm, block_ref, sems.at[comps])
+    block_copy.start()
     copies = [pltpu.make_async_copy(v_hbm.at[c], v_ref.at[c], sems.at[c]) for c in range(comps)]
-    block_copy = pltpu.make_async_copy(block_hbm, block_ref, sems.at[comps])
-    copies[0].start()
-    block_copy.start()
-    for copy in copies[1:]:
+    for copy in copies:
         copy.start()
 
-    def split_right(c):
-        for start in range(0, lines, CHUNK):
-            at = slice(start, start + CHUNK)
-            v = v_ref[c, :, at]
-            edge_0, edge_1 = v[0:1], v[CELLS - 1 : CELLS]
-            below_1 = jnp.concatenate([edge_0, v[: CELLS - 1]], 0)
-            below_2 = jnp.concatenate([edge_0, edge_0, v[: CELLS - 2]], 0)
-            above_1 = jnp.concatenate([v[1:], edge_1], 0)
-            above_2 = jnp.concatenate([v[2:], edge_1, edge_1], 0)
-            right = NEAR_WEIGHT * (above_1 - below_1) + FAR_WEIGHT * (above_2 - below_2)
-            for i, part in enumerate(parts_of(right)):
-                part_ref[c, i * CELLS : (i + 1) * CELLS, at] = part
-
-    row8 = lax.broadcasted_iota(jnp.int32, (8, CHUNK), 0)
-
-    def multiply(c, squares):
-        for start in range(0, lines, CHUNK):
-            at = slice(start, start + CHUNK)
-            high = part_ref[c, 0:CELLS, at]
-            middle = part_ref[c, CELLS : 2 * CELLS, at]
-            low = part_ref[c, 2 * CELLS : 3 * CELLS, at]
-            stacked = jnp.concatenate([high, high, high, middle, middle, low], 0)
-            out = jnp.dot(mat_ref[...], stacked, preferred_element_type=F32)
-            g = out[0:CELLS]
-            g_ref[c, :, at] = g
-            square = g * g
-            tiles = [square[8 * i : 8 * i + 8] for i in range(CELLS // 8)]
-            while len(tiles) > 1:
-                tiles = [x + y for x, y in zip(tiles[0::2], tiles[1::2])]
-            squares = squares + tiles[0]
-            rows = out[CELLS : CELLS + 8]
-            rows = jnp.where((row8 == 4) | (row8 == 5), pltpu.roll(v_ref[c, 0:8, at], 4, 0), rows)
-            rows = jnp.where(row8 >= 6, v_ref[c, CELLS - 8 : CELLS, at], rows)
-            for j in range(CHUNK // LANES):
-                to = stride * (start // LANES + j) + 8 * c
-                send_ref[to : to + 8, :] = rows[:, j * LANES : (j + 1) * LANES]
-        return squares
-
-    copies[0].wait()
-    split_right(0)
-    copies[1].wait()
+    pad_ref[...] = jnp.zeros(pad_ref.shape, F32)
     block_copy.wait()
-    pad_ref[...] = jnp.zeros(pad_ref.shape, F32)
     pad_ref[0:inner, 0:inner] = block_ref[:, 0, :]
     padded = pltpu.roll(pltpu.roll(pad_ref[...], 1, 0), 1, 1)
     first = jnp.broadcast_to(COUPLING * padded[:, 1:2], (CELLS, LANES))
@@ -112,18 +70,34 @@
     matrix = jnp.concatenate([padded, extra], 0)
     high, middle, low = parts_of(matrix[:, 0:CELLS])
     mat_ref[...] = jnp.concatenate([high, middle, low, high, middle, high], 1)
-    split_right(1)
-    squares = multiply(0, jnp.zeros((8, CHUNK), F32))
-    for c in range(2, comps):
+
+    row8 = lax.broadcasted_iota(jnp.int32, (8, CHUNK), 0)
+    energy = jnp.zeros((1, LANES), F32)
+    for c in range(comps):
         copies[c].wait()
-        split_right(c)
-        squares = multiply(c - 1, squares)
-    squares = multiply(comps - 1, squares)
-
-    energy = squares[:, 0:LANES]
-    for j in range(1, CHUNK // LANES):
-        energy = energy + squares[:, j * LANES : (j + 1) * LANES]
-    energy = jnp.sum(energy, axis=0, keepdims=True)
+        for start in range(0, lines, CHUNK):
+            v = v_ref[c, :, start : start + CHUNK]
+            edge_0, edge_1 = v[0:1], v[CELLS - 1 : CELLS]
+            below_1 = jnp.concatenate([edge_0, v[: CELLS - 1]], 0)
+            below_2 = jnp.concatenate([edge_0, edge_0, v[: CELLS - 2]], 0)
+            above_1 = jnp.concatenate([v[1:], edge_1], 0)
+            above_2 = jnp.concatenate([v[2:], edge_1, edge_1], 0)
+            right = NEAR_WEIGHT * (above_1 - below_1) + FAR_WEIGHT * (above_2 - below_2)
+            high, middle, low = parts_of(right)
+            stacked = jnp.concatenate([high, high, high, middle, middle, low], 0)
+            out = jnp.dot(mat_ref[...], stacked, preferred_element_type=F32)
+            g = out[0:CELLS]
+            g_ref[c, :, start : start + CHUNK] = g
+            squares = jnp.sum(g * g, axis=0, keepdims=True)
+            rows = out[CELLS : CELLS + 8]
+            rows = jnp.where((row8 == 4) | (row8 == 5), pltpu.roll(v[0:8], 4, 0), rows)
+            rows = jnp.where(row8 >= 6, v[CELLS - 8 : CELLS], rows)
+            for j in range(CHUNK // LANES):
+                at = slice(j * LANES, (j + 1) * LANES)
+                energy = energy + squares[:, at]
+                to = stride * (start // LANES + j) + 8 * c
+                send_ref[to : to + 8, :] = rows[:, at]
+
     coefs = energy + pltpu.roll(energy, LANES // 2, 1)
     numbers = [
         first[1:2],
@@ -271,23 +245,15 @@
     return found
 
 
-def join_kernel(own_ref, near_ref, far_ref, state_ref, open_ref, send_ref, all_ref):
+def join_kernel(all_ref, state_ref, open_ref, send_ref):
     width = state_ref.shape[2]
     comps = width // LANES
     group = lax.axis_index("gx") // GROUP
-    all_ref[0] = own_ref[...]
-    all_ref[1] = near_ref[...]
-    all_ref[2] = far_ref[1]
-    all_ref[3] = far_ref[0]
 
     def wide(x):
         return tiled(x, comps)
 
-    tile = []
-    for t in range(GROUPS):
-        own = group % 4
-        slot = jnp.where(own >= 2, (t // 2) ^ 1, t // 2) * 2 + jnp.where(own % 2 == 1, (t % 2) ^ 1, t % 2)
-        tile.append(all_ref[slot])
+    tile = [all_ref[t] for t in range(GROUPS)]
     data = [[m[r : r + 1, 0:width] for r in range(8)] for m in tile]
     scal = [[m[r : r + 1, width:] for r in range(8)] for m in tile]
     x_f, x_l, line_a, line_c, v_0, v_1, v_62, v_63 = [[d[r] for d in data] for r in range(8)]
@@ -358,12 +324,14 @@
     out_ref[...] = jnp.broadcast_to(jnp.sum(energy, axis=0, keepdims=True), out_ref.shape)
 
 
-def final_kernel(scale, recv_ref, energy_ref, g_ref, p_ref, q_ref, out_hbm, mean_ref, out_ref, sems):
+def final_kernel(scale, recv_ref, energy_ref, g_ref, p_ref, q_ref, out_hbm, mean_hbm, out_ref, mean_ref, sems):
     comps, _, lines = g_ref.shape
     stride = recv_ref.shape[0] // GROUP
     row8 = lax.broadcasted_iota(jnp.int32, (8, LANES), 0)
     first, last = p_ref[...], q_ref[...]
-    copies = []
+    mean_ref[0, 0] = jnp.sum(energy_ref[...]) * scale
+    copies = [pltpu.make_async_copy(mean_ref, mean_hbm, sems.at[comps])]
+    copies[0].start()
     for c in range(comps):
         for j in range(GROUP):
             at = slice(j * LANES, (j + 1) * LANES)
@@ -376,7 +344,6 @@
         copy = pltpu.make_async_copy(out_ref.at[c], out_hbm.at[c], sems.at[c])
         copy.start()
         copies.append(copy)
-    mean_ref[0, 0] = jnp.sum(energy_ref[...]) * scale
     for copy in copies:
         copy.wait()
 
@@ -407,7 +374,6 @@
             pltpu.VMEM((cells + 16, 6 * cells), BF16),
             pltpu.VMEM((cells, LANES), F32),
             pltpu.VMEM((cells - 2, 1, cells - 2), F32),
-            pltpu.VMEM((comps, 3 * cells, lines), BF16),
             pltpu.SemaphoreType.DMA((comps + 1,)),
         ],
         compiler_params=LARGE,
@@ -433,21 +399,18 @@
         name="group_solve",
     )(recv)
 
-    def swapped(value, mask):
-        pairs = [
-            (t * GROUP + i, (t ^ mask) * GROUP + i) for t in range(GROUPS) for i in range(GROUP)
-        ]
-        return lax.ppermute(value, "gx", pairs)
-
-    near = swapped(msg, 1)
-    far = swapped(jnp.stack([msg, near]), 3)
+    def joined(value, pairs):
+        members = [[GROUP * t + i for t in pair] for pair in pairs for i in range(GROUP)]
+        return lax.all_gather(value, "gx", axis_index_groups=members)
+
+    near = joined(msg, ((0, 1), (2, 3)))
+    every = joined(near, ((0, 3), (1, 2))).reshape(GROUPS, 8, width + LANES)
     send_back = pl.pallas_call(
         join_kernel,
         out_shape=shape((GROUP * back_rows, LANES)),
-        scratch_shapes=[pltpu.VMEM((GROUPS, 8, width + LANES), F32)],
         compiler_params=SMALL,
         name="join_groups",
-    )(msg, near, far, state, opened)
+    )(every, state, opened)
     back = spread(send_back, "gx", axis_index_groups=groups)
     energy = pl.pallas_call(
         energy_kernel,
@@ -460,14 +423,12 @@
     derivative, mean_square = pl.pallas_call(
         functools.partial(final_kernel, 1.0 / total_count),
         in_specs=[pl.BlockSpec(memory_space=pltpu.VMEM)] * 5,
-        out_specs=[
-            pl.BlockSpec(memory_space=pltpu.HBM),
-            pl.BlockSpec(memory_space=pltpu.SMEM),
-        ],
+        out_specs=[pl.BlockSpec(memory_space=pltpu.HBM)] * 2,
         out_shape=[shape((comps, cells, lines)), shape((1, 1))],
         scratch_shapes=[
             pltpu.VMEM((comps, cells, lines), F32),
-            pltpu.SemaphoreType.DMA((comps,)),
+            pltpu.SMEM((1, 1), F32),
+            pltpu.SemaphoreType.DMA((comps + 1,)),
         ],
         compiler_params=LARGE,
         name="final_update",

time: 68.6 us -> 65.1 us (0.949)
  blocking collectives: 42.6 us -> 59.6 us
  starting transfers between devices: 17 us -> 0 us
  waiting for transfers between devices: 2.4 us -> 0 us
  Pallas kernels: 5.57 us -> 4.67 us
    ppermute x2 -> x0, starting transfers between devices: 17 us -> none  [swapped(): return lax.ppermute(value, 'gx', pairs)]
    all_gather x0 -> x2, blocking collectives: none -> 17 us  [joined(): return lax.all_gather(value, 'gx', axis_index_groups=members)]
    ppermute x2 -> x0, waiting for transfers between devices: 2.4 us -> none  [swapped(): return lax.ppermute(value, 'gx', pairs)]
  transfers between devices with their start and end apart: 2 -> 0, of which waited for: 2 -> 0; matrix products, arithmetic and copies ran while one was open for 0% -> 0% of each run, Pallas kernels for 0% -> 0%
where the time goes in v4:
time: 65.1 us; the launch traced here: 64.9 us
  blocking collectives  59.6 us (92%)
  Pallas kernels  4.67 us (7%)
    all_to_all x3, blocking collectives, spread(): lax.all_to_all(rows, axis, 0, 0, tiled=True, **kwargs).reshape(value.shape)  42.6 us
    all_gather x2, blocking collectives, joined(): return lax.all_gather(value, 'gx', axis_index_groups=members)  17 us
    pallas_call x1, Pallas kernels, on_device(): pl.pallas_call(local_kernel, in_specs=[pl.BlockSpec(memory_space=pltpu.HB...  2.9 us

profile of v4, /device:TPU:1, one launch (start us, length us, event | category | flops | bytes accessed | tf_op | source)
XLA Modules:
  0.0 64.9 jit_solution(5013672971858157488)
XLA Ops:
  0.6 2.9 %local_solve.1 = (f32[3,64,2048]{2,1,0:T(8,128)S(1)}, f32[400,128]{1,0:T(8,128)S(1)}, f32[64,128]{1,0:T(8,128)S(1)}, f32[64,128]{1,0:T(8,128)S(1)}) custom-call(f32[3,64,2048]{2,1,0:T(8,128)} %v_hbm.1, f32[62,1,62]{2,1,0:T(1,128)} %bitcast.23), custom_call_target="tpu_custom_call" | custom-call | tf_op jit(solution)/shard_map/local_solve/pallas_call | solution.py:359
  3.5 17.5 %all_to_all.15 = f32[400,1,128]{2,1,0:T(1,128)S(1)} all-to-all(f32[400,1,128]{2,1,0:T(1,128)S(1)} %bitcast.19), channel_id=1, replica_groups={{0,8,16,24,32,40,48,56,64,72,80,88,96,104,112,120},{128,136,144,152,160..., dimensions={0} | all-to-all | bytes 409600 | tf_op jit(solution)/shard_map/all_to_all | solution.py:388
  21.1 0.3 group_solve.1
  21.3 8.7 %all-gather = f32[16,512]{1,0:T(8,128)S(1)} all-gather(f32[8,512]{1,0:T(8,128)S(1)} %get-tuple-element.12), channel_id=2, replica_groups={{0,128},{8,136},{16,144},{24,152},{32,160},{40,168},{48,176},{56,184},{..., dimensions={0}, use_global_device_ids=true | all-gather | bytes 49152 | tf_op jit(solution)/shard_map/all_gather | solution.py:404
  30.0 8.3 %all-gather.1.all_ref = f32[4,8,512]{2,1,0:T(8,128)S(1)} all-gather(f32[2,8,512]{2,1,0:T(8,128)S(1)} %bitcast.22), channel_id=3, replica_groups={{0,384},{8,392},{16,400},{24,408},{32,416},{40,424},{48,432},{56,440},{..., dimensions={0}, use_global_device_ids=true | all-gather | bytes 98304 | tf_op jit(solution)/shard_map/all_gather | solution.py:404
  38.3 0.2 join_groups.1
  38.5 12.2 %all_to_all.16 = f32[208,1,128]{2,1,0:T(1,128)S(1)} all-to-all(f32[208,1,128]{2,1,0:T(1,128)S(1)} %bitcast.18), channel_id=1, replica_groups={{0,8,16,24,32,40,48,56,64,72,80,88,96,104,112,120},{128,136,144,152,160..., dimensions={0} | all-to-all | bytes 212992 | tf_op jit(solution)/shard_map/all_to_all | solution.py:388
  50.8 12.8 %all_to_all.17 = f32[8,1,128]{2,1,0:T(1,128)S(1)} all-to-all(f32[8,1,128]{2,1,0:T(1,128)S(1)} %bitcast.21), channel_id=1, replica_groups=mesh['gx'=64,'yz'=8] {'yz'}, dimensions={0} | all-to-all | bytes 8192 | tf_op jit(solution)/shard_map/all_to_all | solution.py:388
  63.6 1.3 %final_update.1 = (f32[3,64,2048]{2,1,0:T(8,128)}, f32[1,1]{1,0:T(1,128)}) custom-call(f32[208,128]{1,0:T(8,128)S(1)} %bitcast.16, f32[8,128]{1,0:T(8,128)S(1)} %bitcast.20, f32[3,64,2048]{2,1,0:T(8,128)S(1)} %get-tuple-element.15.g_ref, f32[64,128]{1,0:T(8,128)S(1)} %get-tuple-element.16.p_ref, f32[64,128]{1,0:T(8,128)S(1)} %get-tuple-element.17.q_ref), custom_call_target="tpu_custom_call" | custom-call | tf_op jit(solution)/shard_map/final_update/pallas_call | solution.py:423
  (1 shorter events, 0.0 us)

commit v5 on v4

--- a/solution.py
+++ b/solution.py
@@ -68,6 +68,8 @@
     extra = jnp.where(rows == 2, first_sum, extra)
     extra = jnp.where(rows == 3, last_sum, extra)
     matrix = jnp.concatenate([padded, extra], 0)
+    beside = pltpu.roll(matrix, 1, 1) + pltpu.roll(matrix, LANES - 1, 1)
+    matrix = NEAR_WEIGHT * matrix + FAR_WEIGHT * beside
     high, middle, low = parts_of(matrix[:, 0:CELLS])
     mat_ref[...] = jnp.concatenate([high, middle, low, high, middle, high], 1)
 
@@ -78,12 +80,9 @@
         for start in range(0, lines, CHUNK):
             v = v_ref[c, :, start : start + CHUNK]
             edge_0, edge_1 = v[0:1], v[CELLS - 1 : CELLS]
-            below_1 = jnp.concatenate([edge_0, v[: CELLS - 1]], 0)
-            below_2 = jnp.concatenate([edge_0, edge_0, v[: CELLS - 2]], 0)
-            above_1 = jnp.concatenate([v[1:], edge_1], 0)
-            above_2 = jnp.concatenate([v[2:], edge_1, edge_1], 0)
-            right = NEAR_WEIGHT * (above_1 - below_1) + FAR_WEIGHT * (above_2 - below_2)
-            high, middle, low = parts_of(right)
+            below = jnp.concatenate([edge_0, v[: CELLS - 1]], 0)
+            above = jnp.concatenate([v[1:], edge_1], 0)
+            high, middle, low = parts_of(above - below)
             stacked = jnp.concatenate([high, high, high, middle, middle, low], 0)
             out = jnp.dot(mat_ref[...], stacked, preferred_element_type=F32)
             g = out[0:CELLS]
@@ -253,7 +252,7 @@
     def wide(x):
         return tiled(x, comps)
 
-    tile = [all_ref[t] for t in range(GROUPS)]
+    tile = [all_ref[(0, 2, 3, 1)[t]] for t in range(GROUPS)]
     data = [[m[r : r + 1, 0:width] for r in range(8)] for m in tile]
     scal = [[m[r : r + 1, width:] for r in range(8)] for m in tile]
     x_f, x_l, line_a, line_c, v_0, v_1, v_62, v_63 = [[d[r] for d in data] for r in range(8)]
@@ -318,20 +317,12 @@
     send_ref[pl.ds(4 * comps, GROUP, stride=stride), :] = jnp.broadcast_to(energy, (GROUP, LANES))
 
 
-def energy_kernel(recv_ref, out_ref):
-    stride = recv_ref.shape[0] // GROUP
-    energy = recv_ref[pl.ds(stride - 1, GROUP, stride=stride), :]
-    out_ref[...] = jnp.broadcast_to(jnp.sum(energy, axis=0, keepdims=True), out_ref.shape)
-
-
-def final_kernel(scale, recv_ref, energy_ref, g_ref, p_ref, q_ref, out_hbm, mean_hbm, out_ref, mean_ref, sems):
+def update_cells(recv_ref, g_ref, p_ref, q_ref, out_hbm, out_ref, sems):
     comps, _, lines = g_ref.shape
     stride = recv_ref.shape[0] // GROUP
     row8 = lax.broadcasted_iota(jnp.int32, (8, LANES), 0)
     first, last = p_ref[...], q_ref[...]
-    mean_ref[0, 0] = jnp.sum(energy_ref[...]) * scale
-    copies = [pltpu.make_async_copy(mean_ref, mean_hbm, sems.at[comps])]
-    copies[0].start()
+    copies = []
     for c in range(comps):
         for j in range(GROUP):
             at = slice(j * LANES, (j + 1) * LANES)
@@ -348,6 +339,36 @@
         copy.wait()
 
 
+def early_device():
+    place = lax.axis_index("yz")
+    return (place % 2 == 1) | (place == 0)
+
+
+def early_kernel(recv_ref, g_ref, p_ref, q_ref, out_hbm, energy_ref, out_ref, sems):
+    stride = recv_ref.shape[0] // GROUP
+    energy = recv_ref[pl.ds(stride - 1, GROUP, stride=stride), :]
+    energy_ref[...] = jnp.broadcast_to(jnp.sum(energy, axis=0, keepdims=True), energy_ref.shape)
+
+    @pl.when(early_device())
+    def _():
+        update_cells(recv_ref, g_ref, p_ref, q_ref, out_hbm, out_ref, sems)
+
+
+def late_kernel(
+    scale, begun_hbm, energy_ref, recv_ref, g_ref, p_ref, q_ref, out_hbm, mean_hbm, mean_ref, out_ref, sems
+):
+    comps = g_ref.shape[0]
+    mean_ref[0, 0] = jnp.sum(energy_ref[...]) * scale
+    mean_copy = pltpu.make_async_copy(mean_ref, mean_hbm, sems.at[comps])
+    mean_copy.start()
+
+    @pl.when(jnp.logical_not(early_device()))
+    def _():
+        update_cells(recv_ref, g_ref, p_ref, q_ref, out_hbm, out_ref, sems)
+
+    mean_copy.wait()
+
+
 def on_device(velocity, blocks):
     comps, cells, lines = velocity.shape
     width = comps * LANES
@@ -403,8 +424,8 @@
         members = [[GROUP * t + i for t in pair] for pair in pairs for i in range(GROUP)]
         return lax.all_gather(value, "gx", axis_index_groups=members)
 
-    near = joined(msg, ((0, 1), (2, 3)))
-    every = joined(near, ((0, 3), (1, 2))).reshape(GROUPS, 8, width + LANES)
+    near = joined(msg, ((0, 3), (1, 2)))
+    every = joined(near, ((0, 1), (3, 2))).reshape(GROUPS, 8, width + LANES)
     send_back = pl.pallas_call(
         join_kernel,
         out_shape=shape((GROUP * back_rows, LANES)),
@@ -412,27 +433,38 @@
         name="join_groups",
     )(every, state, opened)
     back = spread(send_back, "gx", axis_index_groups=groups)
-    energy = pl.pallas_call(
-        energy_kernel,
-        out_shape=shape((yz_count, LANES)),
-        compiler_params=SMALL,
-        name="line_energy",
-    )(back)
+    begun, energy = pl.pallas_call(
+        early_kernel,
+        in_specs=[pl.BlockSpec(memory_space=pltpu.VMEM)] * 4,
+        out_specs=[
+            pl.BlockSpec(memory_space=pltpu.HBM),
+            pl.BlockSpec(memory_space=pltpu.VMEM),
+        ],
+        out_shape=[shape((comps, cells, lines)), shape((yz_count, LANES))],
+        scratch_shapes=[
+            pltpu.VMEM((comps, cells, lines), F32),
+            pltpu.SemaphoreType.DMA((comps,)),
+        ],
+        compiler_params=LARGE,
+        name="early_update",
+    )(back, g, p_rows, q_rows)
     energies = spread(energy, "yz")
     total_count = comps * cells * lines * lax.axis_size("gx") * yz_count
     derivative, mean_square = pl.pallas_call(
-        functools.partial(final_kernel, 1.0 / total_count),
-        in_specs=[pl.BlockSpec(memory_space=pltpu.VMEM)] * 5,
+        functools.partial(late_kernel, 1.0 / total_count),
+        in_specs=[pl.BlockSpec(memory_space=pltpu.HBM)]
+        + [pl.BlockSpec(memory_space=pltpu.VMEM)] * 5,
         out_specs=[pl.BlockSpec(memory_space=pltpu.HBM)] * 2,
         out_shape=[shape((comps, cells, lines)), shape((1, 1))],
+        input_output_aliases={0: 0},
         scratch_shapes=[
+            pltpu.SMEM((1, 1), F32),
             pltpu.VMEM((comps, cells, lines), F32),
-            pltpu.SMEM((1, 1), F32),
             pltpu.SemaphoreType.DMA((comps + 1,)),
         ],
         compiler_params=LARGE,
-        name="final_update",
-    )(back, energies, g, p_rows, q_rows)
+        name="late_update",
+    )(begun, energies, back, g, p_rows, q_rows)
     return derivative, mean_square[0, 0]
 
 

time: 65.1 us -> 64.1 us (0.985)
  blocking collectives: 59.6 us -> 58.2 us
    all_to_all x3, blocking collectives: 42.6 us -> 41.3 us  [spread(): lax.all_to_all(rows, axis, 0, 0, tiled=True, **kwargs).reshape(value.shape)]
where the time goes in v5:
time: 64.1 us; the launch traced here: 63.8 us
  blocking collectives  58.2 us (91%)
  Pallas kernels  4.95 us (8%)
  between operations  0.65 us (1%)
    all_to_all x3, blocking collectives, spread(): lax.all_to_all(rows, axis, 0, 0, tiled=True, **kwargs).reshape(value.shape)  41.3 us
    all_gather x2, blocking collectives, joined(): return lax.all_gather(value, 'gx', axis_index_groups=members)  17 us
    pallas_call x1, Pallas kernels, on_device(): pl.pallas_call(local_kernel, in_specs=[pl.BlockSpec(memory_space=pltpu.HB...  2.55 us

profile of v5, /device:TPU:1, one launch (start us, length us, event | category | flops | bytes accessed | tf_op | source)
XLA Modules:
  0.0 63.8 jit_solution(9987756131912450713)
XLA Ops:
  0.6 2.6 %local_solve.1 = (f32[3,64,2048]{2,1,0:T(8,128)S(1)}, f32[400,128]{1,0:T(8,128)S(1)}, f32[64,128]{1,0:T(8,128)S(1)}, f32[64,128]{1,0:T(8,128)S(1)}) custom-call(f32[3,64,2048]{2,1,0:T(8,128)} %v_hbm.1, f32[62,1,62]{2,1,0:T(1,128)} %bitcast.23), custom_call_target="tpu_custom_call" | custom-call | tf_op jit(solution)/shard_map/local_solve/pallas_call | solution.py:380
  3.2 17.5 %all_to_all.15 = f32[400,1,128]{2,1,0:T(1,128)S(1)} all-to-all(f32[400,1,128]{2,1,0:T(1,128)S(1)} %bitcast.19), channel_id=1, replica_groups={{0,8,16,24,32,40,48,56,64,72,80,88,96,104,112,120},{128,136,144,152,160..., dimensions={0} | all-to-all | bytes 409600 | tf_op jit(solution)/shard_map/all_to_all | solution.py:409
  20.7 0.3 group_solve.1
  21.0 9.6 %all-gather = f32[16,512]{1,0:T(8,128)S(1)} all-gather(f32[8,512]{1,0:T(8,128)S(1)} %get-tuple-element.14), channel_id=2, replica_groups={{0,384},{8,392},{16,400},{24,408},{32,416},{40,424},{48,432},{56,440},{..., dimensions={0}, use_global_device_ids=true | all-gather | bytes 49152 | tf_op jit(solution)/shard_map/all_gather | solution.py:425
  30.6 7.3 %all-gather.1.all_ref = f32[4,8,512]{2,1,0:T(8,128)S(1)} all-gather(f32[2,8,512]{2,1,0:T(8,128)S(1)} %bitcast.22), channel_id=3, replica_groups={{0,128},{8,136},{16,144},{24,152},{32,160},{40,168},{48,176},{56,184},{..., dimensions={0}, use_global_device_ids=true | all-gather | bytes 98304 | tf_op jit(solution)/shard_map/all_gather | solution.py:425
  37.9 0.2 join_groups.1
  38.1 11.9 %all_to_all.16 = f32[208,1,128]{2,1,0:T(1,128)S(1)} all-to-all(f32[208,1,128]{2,1,0:T(1,128)S(1)} %bitcast.18), channel_id=1, replica_groups={{0,8,16,24,32,40,48,56,64,72,80,88,96,104,112,120},{128,136,144,152,160..., dimensions={0} | all-to-all | bytes 212992 | tf_op jit(solution)/shard_map/all_to_all | solution.py:409
  50.1 1.3 %early_update.1 = (f32[3,64,2048]{2,1,0:T(8,128)}, f32[8,128]{1,0:T(8,128)S(1)}) custom-call(f32[208,128]{1,0:T(8,128)S(1)} %bitcast.15, f32[3,64,2048]{2,1,0:T(8,128)S(1)} %get-tuple-element.17.g_ref, f32[64,128]{1,0:T(8,128)S(1)} %get-tuple-element.18.p_ref, f32[64,128]{1,0:T(8,128)S(1)} %get-tuple-element.19.q_ref), custom_call_target="tpu_custom_call" | custom-call | tf_op jit(solution)/shard_map/early_update/pallas_call | solution.py:436
  51.4 11.8 %all_to_all.17 = f32[8,1,128]{2,1,0:T(1,128)S(1)} all-to-all(f32[8,1,128]{2,1,0:T(1,128)S(1)} %bitcast.21), channel_id=1, replica_groups=mesh['gx'=64,'yz'=8] {'yz'}, dimensions={0} | all-to-all | bytes 8192 | tf_op jit(solution)/shard_map/all_to_all | solution.py:409
  63.2 0.7 %late_update.1 = (f32[3,64,2048]{2,1,0:T(8,128)}, f32[1,1]{1,0:T(1,128)}) custom-call(f32[3,64,2048]{2,1,0:T(8,128)} %get-tuple-element.20.begun_hbm, f32[8,128]{1,0:T(8,128)S(1)} %bitcast.20, f32[208,128]{1,0:T(8,128)S(1)} %bitcast.16, f32[3,64,2048]{2,1,0:T(8,128)S(1)} %get-tuple-element.17.g_ref, ...), custom_call_target="tpu_custom_call", output_to_operand_aliasing={{0}: (0, {})} | custom-call | tf_op jit(solution)/shard_map/late_update/pallas_call | solution.py:453

commit v6 on v5

--- a/solution.py
+++ b/solution.py
@@ -13,6 +13,8 @@
 
 GROUP = 16
 GROUPS = 4
+ORDER = tuple(4 * z + y for y in (2, 3, 1, 0) for z in (2, 1, 3, 0))
+YZ_ORDER = (5, 4, 7, 6, 3, 2, 1, 0)
 LANES = 128
 CELLS = 64
 CHUNK = 512
@@ -114,16 +116,20 @@
         send_ref[to : to + 1, :] = coefs
 
 
-def group_kernel(recv_ref, msg_ref, state_ref, open_ref):
-    stride = recv_ref.shape[0] // GROUP
-    comps = stride // 8
+def group_kernel(recv_ref, msg_ref, state_ref, open_ref, block_ref):
+    count = recv_ref.shape[0] // GROUP
+    stride = block_ref.shape[0] // GROUP
+    comps = count // 8
+    for i, place in enumerate(ORDER):
+        to = stride * place
+        block_ref[to : to + count, :] = recv_ref[count * i : count * (i + 1), :]
     width = comps * LANES
 
     def rows(r):
-        parts = [recv_ref[pl.ds(8 * i + r, GROUP, stride=stride), :] for i in range(comps)]
+        parts = [block_ref[pl.ds(8 * i + r, GROUP, stride=stride), :] for i in range(comps)]
         return jnp.concatenate(parts, 1)
 
-    numbers = recv_ref[pl.ds(8 * comps, GROUP, stride=stride), :]
+    numbers = block_ref[pl.ds(8 * comps, GROUP, stride=stride), :]
 
     def coef(r):
         return jnp.broadcast_to(numbers[:, r : r + 1], (GROUP, LANES))
@@ -244,26 +250,108 @@
     return found
 
 
-def join_kernel(all_ref, state_ref, open_ref, send_ref):
+def unpacked(message, width):
+    return (
+        [message[r : r + 1, 0:width] for r in range(8)],
+        [message[r : r + 1, width:] for r in range(8)],
+    )
+
+
+def pair_kernel(both_ref, msg_ref, state_ref, open_ref):
+    width = both_ref.shape[2] - LANES
+    comps = width // LANES
+
+    def wide(x):
+        return tiled(x, comps)
+
+    left, l = unpacked(both_ref[0], width)
+    right, r = unpacked(both_ref[1], width)
+    x_f, x_l, line_a, line_c, v_0, v_1, v_62, v_63 = [list(p) for p in zip(left, right)]
+    a_f, a_l, c_f, c_l, q_aa, q_ac, q_cc, part = [list(p) for p in zip(l, r)]
+
+    jump = v_63[0] - v_0[1]
+    rhs_c = -COUPLING * x_f[1] - (2.0 / 3.0) * jump + FAR_WEIGHT * (v_1[1] - v_63[0])
+    rhs_a = -COUPLING * x_l[0] - (2.0 / 3.0) * jump - FAR_WEIGHT * (v_62[0] - v_0[1])
+    inverse = 1.0 / (1.0 - (COUPLING * a_f[1]) * (COUPLING * c_l[0]))
+    to_c, to_a = COUPLING * a_f[1] * inverse, COUPLING * c_l[0] * inverse
+    c_0 = wide(inverse) * rhs_c - wide(to_c) * rhs_a
+    c_alpha = to_c * (COUPLING * a_l[0])
+    c_gamma = -inverse * (COUPLING * c_f[1])
+    a_0 = wide(inverse) * rhs_a - wide(to_a) * rhs_c
+    a_alpha = -inverse * (COUPLING * a_l[0])
+    a_gamma = to_a * (COUPLING * c_f[1])
+
+    d = jump * (1.0 / 12.0)
+    inner_u = x_f[1] + wide(a_f[1]) * a_0
+    inner_w = x_l[0] + wide(c_l[0]) * c_0
+    both_alpha = a_f[1] * a_alpha + a_l[0] + c_l[0] * c_alpha
+    both_gamma = a_f[1] * a_gamma + c_f[1] + c_l[0] * c_gamma
+    slope_c = line_c[0] + wide(2.0 * q_cc[0]) * c_0
+    slope_a = line_a[1] + wide(2.0 * q_aa[1]) * a_0
+    line_alpha = line_a[0] + wide(2.0 * q_ac[0]) * c_0 + wide(c_alpha) * slope_c
+    line_alpha = line_alpha + wide(a_alpha) * slope_a - wide(2.0 * both_alpha) * d
+    line_gamma = line_c[1] + wide(2.0 * q_ac[1]) * a_0 + wide(a_gamma) * slope_a
+    line_gamma = line_gamma + wide(c_gamma) * slope_c - wide(2.0 * both_gamma) * d
+    base = c_0 * (line_c[0] + wide(q_cc[0]) * c_0) + a_0 * (line_a[1] + wide(q_aa[1]) * a_0)
+    base = base + 2.0 * d * (d - inner_u - inner_w)
+    total = part[0] + part[1]
+    for i in range(comps):
+        total = total + base[:, i * LANES : (i + 1) * LANES]
+    q_alpha = q_aa[0] + c_alpha * (2.0 * q_ac[0] + q_cc[0] * c_alpha) + q_aa[1] * a_alpha * a_alpha
+    q_gamma = q_cc[1] + a_gamma * (2.0 * q_ac[1] + q_aa[1] * a_gamma) + q_cc[0] * c_gamma * c_gamma
+    q_mixed = c_gamma * (q_ac[0] + q_cc[0] * c_alpha) + a_alpha * (q_ac[1] + q_aa[1] * a_gamma)
+
+    msg_ref[:, 0:width] = jnp.concatenate(
+        [
+            x_f[0] + wide(c_f[0]) * c_0,
+            x_l[1] + wide(a_l[1]) * a_0,
+            line_alpha,
+            line_gamma,
+            v_0[0],
+            v_1[0],
+            v_62[1],
+            v_63[1],
+        ],
+        0,
+    )
+    msg_ref[:, width:] = jnp.concatenate(
+        [
+            a_f[0] + c_f[0] * c_alpha,
+            a_l[1] * a_alpha,
+            c_f[0] * c_gamma,
+            c_l[1] + a_l[1] * a_gamma,
+            q_alpha,
+            q_mixed,
+            q_gamma,
+            total,
+        ],
+        0,
+    )
+    none = jnp.zeros_like(jump)
+    state_ref[...] = jnp.concatenate([c_0, a_0, jump] + [none] * 5, 0)
+    none = jnp.zeros_like(inverse)
+    open_ref[...] = jnp.concatenate([c_alpha, c_gamma, a_alpha, a_gamma] + [none] * 4, 0)
+
+
+def join_kernel(all_ref, pair_ref, pair_open_ref, state_ref, open_ref, send_ref, block_ref):
     width = state_ref.shape[2]
     comps = width // LANES
     group = lax.axis_index("gx") // GROUP
+    pairs = all_ref.shape[0]
 
     def wide(x):
         return tiled(x, comps)
 
-    tile = [all_ref[(0, 2, 3, 1)[t]] for t in range(GROUPS)]
-    data = [[m[r : r + 1, 0:width] for r in range(8)] for m in tile]
-    scal = [[m[r : r + 1, width:] for r in range(8)] for m in tile]
+    data, scal = zip(*[unpacked(all_ref[t], width) for t in range(pairs)])
     x_f, x_l, line_a, line_c, v_0, v_1, v_62, v_63 = [[d[r] for d in data] for r in range(8)]
     a_f, a_l, c_f, c_l, q_aa, q_ac, q_cc, part = [[s[r] for s in scal] for r in range(8)]
 
     one = jnp.ones((1, LANES), F32)
-    jump = [v_63[t - 1] - v_0[t] for t in range(GROUPS)]
+    jump = [v_63[t - 1] - v_0[t] for t in range(pairs)]
     matrix, rhs = [], []
-    for t in range(GROUPS):
-        before, after = (t - 1) % GROUPS, (t + 1) % GROUPS
-        row_a, row_c = [None] * (2 * GROUPS), [None] * (2 * GROUPS)
+    for t in range(pairs):
+        before, after = (t - 1) % pairs, (t + 1) % pairs
+        row_a, row_c = [None] * (2 * pairs), [None] * (2 * pairs)
         row_a[2 * t] = one
         row_a[2 * before] = COUPLING * a_l[before]
         row_a[2 * before + 1] = COUPLING * c_l[before]
@@ -281,9 +369,9 @@
     value_a, value_c = found[0::2], found[1::2]
 
     energy = jnp.zeros((1, LANES), F32)
-    for t in range(GROUPS):
+    for t in range(pairs):
         a, c = value_a[t], value_c[t]
-        after = (t + 1) % GROUPS
+        after = (t + 1) % pairs
         u_end = x_f[t] + wide(a_f[t]) * a + wide(c_f[t]) * c
         w_end = x_l[t] + wide(a_l[t]) * a + wide(c_l[t]) * c
         d_l, d_r = jump[t] * (1.0 / 12.0), jump[after] * (1.0 / 12.0)
@@ -294,14 +382,20 @@
         for i in range(comps):
             energy = energy + lines[:, i * LANES : (i + 1) * LANES]
 
+    first_pair = (group == 0) | (group == 3)
+    on_left = (group == 3) | (group == 1)
+
     def mine(values):
-        result = values[0]
-        for t in range(1, GROUPS):
-            result = jnp.where(group == t, values[t], result)
-        return result
-
-    a, c = mine(value_a), mine(value_c)
-    left, right = mine(jump), mine(jump[1:] + jump[:1])
+        return jnp.where(first_pair, values[0], values[1])
+
+    alpha, gamma = mine(value_a), mine(value_c)
+    inner = [pair_ref[r : r + 1, :] for r in range(3)]
+    slope = [wide(pair_open_ref[r : r + 1, :]) for r in range(4)]
+    inner_c = inner[0] + slope[0] * alpha + slope[1] * gamma
+    inner_a = inner[1] + slope[2] * alpha + slope[3] * gamma
+    a, c = jnp.where(on_left, alpha, inner_a), jnp.where(on_left, inner_c, gamma)
+    left = jnp.where(on_left, mine(jump), inner[2])
+    right = jnp.where(on_left, inner[2], mine(jump[1:] + jump[:1]))
     seg = lax.broadcasted_iota(jnp.int32, (GROUP, width), 0)
     u_t = state_ref[0] + wide(open_ref[0]) * a + wide(open_ref[2]) * c
     w_t = state_ref[1] + wide(open_ref[1]) * a + wide(open_ref[3]) * c
@@ -309,12 +403,15 @@
     jump_r = jnp.where(seg == GROUP - 1, right, state_ref[3])
     u = u_t - jump_l * (1.0 / 12.0)
     w = w_t - jump_r * (1.0 / 12.0)
-    stride = send_ref.shape[0] // GROUP
+    count = send_ref.shape[0] // GROUP
+    stride = block_ref.shape[0] // GROUP
     for i in range(comps):
         for r, value in enumerate((u_t, w_t, u, w)):
             part_i = value[:, i * LANES : (i + 1) * LANES]
-            send_ref[pl.ds(4 * i + r, GROUP, stride=stride), :] = part_i
-    send_ref[pl.ds(4 * comps, GROUP, stride=stride), :] = jnp.broadcast_to(energy, (GROUP, LANES))
+            block_ref[pl.ds(4 * i + r, GROUP, stride=stride), :] = part_i
+    block_ref[pl.ds(4 * comps, GROUP, stride=stride), :] = jnp.broadcast_to(energy, (GROUP, LANES))
+    for i, place in enumerate(ORDER):
+        send_ref[count * i : count * (i + 1), :] = block_ref[stride * place : stride * place + count, :]
 
 
 def update_cells(recv_ref, g_ref, p_ref, q_ref, out_hbm, out_ref, sems):
@@ -374,7 +471,7 @@
     width = comps * LANES
     send_rows, back_rows = 8 * comps + 1, 4 * comps + 1
     yz_count = lax.axis_size("yz")
-    groups = [[GROUP * t + i for i in range(GROUP)] for t in range(GROUPS)]
+    groups = [[GROUP * t + i for i in ORDER] for t in range(GROUPS)]
     shape = functools.partial(jax.ShapeDtypeStruct, dtype=F32)
 
     g, send, p_rows, q_rows = pl.pallas_call(
@@ -416,6 +513,7 @@
             shape((4, GROUP, width)),
             shape((4, GROUP, LANES)),
         ],
+        scratch_shapes=[pltpu.VMEM((GROUP * 8 * (comps + 1), LANES), F32)],
         compiler_params=SMALL,
         name="group_solve",
     )(recv)
@@ -424,14 +522,21 @@
         members = [[GROUP * t + i for t in pair] for pair in pairs for i in range(GROUP)]
         return lax.all_gather(value, "gx", axis_index_groups=members)
 
-    near = joined(msg, ((0, 3), (1, 2)))
-    every = joined(near, ((0, 1), (3, 2))).reshape(GROUPS, 8, width + LANES)
+    near = joined(msg, ((3, 0), (1, 2)))
+    pair_msg, pair_state, pair_open = pl.pallas_call(
+        pair_kernel,
+        out_shape=[shape((8, width + LANES)), shape((8, width)), shape((8, LANES))],
+        compiler_params=SMALL,
+        name="pair_groups",
+    )(near)
+    every = joined(pair_msg, ((0, 1), (3, 2)))
     send_back = pl.pallas_call(
         join_kernel,
         out_shape=shape((GROUP * back_rows, LANES)),
+        scratch_shapes=[pltpu.VMEM((GROUP * -(-back_rows // 8) * 8, LANES), F32)],
         compiler_params=SMALL,
         name="join_groups",
-    )(every, state, opened)
+    )(every, pair_state, pair_open, state, opened)
     back = spread(send_back, "gx", axis_index_groups=groups)
     begun, energy = pl.pallas_call(
         early_kernel,
@@ -448,7 +553,7 @@
         compiler_params=LARGE,
         name="early_update",
     )(back, g, p_rows, q_rows)
-    energies = spread(energy, "yz")
+    energies = spread(energy, "yz", axis_index_groups=[YZ_ORDER])
     total_count = comps * cells * lines * lax.axis_size("gx") * yz_count
     derivative, mean_square = pl.pallas_call(
         functools.partial(late_kernel, 1.0 / total_count),

time: 64.1 us -> 58.5 us (0.913)
  blocking collectives: 58.2 us -> 52.5 us
    all_to_all x3, blocking collectives: 41.3 us -> 35.2 us  [spread(): lax.all_to_all(rows, axis, 0, 0, tiled=True, **kwargs).reshape(value.shape)]
where the time goes in v6:
time: 58.5 us; the launch traced here: 58.2 us
  blocking collectives  52.5 us (90%)
  Pallas kernels  5.04 us (9%)
  between operations  0.67 us (1%)
    all_to_all x3, blocking collectives, spread(): lax.all_to_all(rows, axis, 0, 0, tiled=True, **kwargs).reshape(value.shape)  35.2 us
    all_gather x2, blocking collectives, joined(): return lax.all_gather(value, 'gx', axis_index_groups=members)  17.4 us
    pallas_call x1, Pallas kernels, on_device(): pl.pallas_call(local_kernel, in_specs=[pl.BlockSpec(memory_space=pltpu.HB...  2.55 us
    pallas_call x1, Pallas kernels, on_device(): pl.pallas_call(early_kernel, in_specs=[pl.BlockSpec(memory_space=pltpu.VM...  1.27 us

profile of v6, /device:TPU:1, one launch (start us, length us, event | category | flops | bytes accessed | tf_op | source)
XLA Modules:
  0.0 58.2 jit_solution(1923395058666416939)
XLA Ops:
  0.6 2.6 %local_solve.1 = (f32[3,64,2048]{2,1,0:T(8,128)S(1)}, f32[400,128]{1,0:T(8,128)S(1)}, f32[64,128]{1,0:T(8,128)S(1)}, f32[64,128]{1,0:T(8,128)S(1)}) custom-call(f32[3,64,2048]{2,1,0:T(8,128)} %v_hbm.1, f32[62,1,62]{2,1,0:T(1,128)} %bitcast.25), custom_call_target="tpu_custom_call" | custom-call | tf_op jit(solution)/shard_map/local_solve/pallas_call | solution.py:477
  3.2 13.6 %all_to_all.15 = f32[400,1,128]{2,1,0:T(1,128)S(1)} all-to-all(f32[400,1,128]{2,1,0:T(1,128)S(1)} %bitcast.20), channel_id=1, replica_groups={{80,48,112,16,88,56,120,24,72,40,104,8,64,32,96,0},{208,176,240,144,216..., dimensions={0} | all-to-all | bytes 409600 | tf_op jit(solution)/shard_map/all_to_all | solution.py:506
  16.8 0.3 group_solve.1
  17.1 10.2 %all-gather = f32[16,512]{1,0:T(8,128)S(1)} all-gather(f32[8,512]{1,0:T(8,128)S(1)} %get-tuple-element.17), channel_id=2, replica_groups={{384,0},{392,8},{400,16},{408,24},{416,32},{424,40},{432,48},{440,56},{..., dimensions={0}, use_global_device_ids=true | all-gather | bytes 49152 | tf_op jit(solution)/shard_map/all_gather | solution.py:523
  27.3 0.1 pair_groups.1
  27.4 7.2 %all-gather.1 = f32[16,512]{1,0:T(8,128)S(1)} all-gather(f32[8,512]{1,0:T(8,128)S(1)} %get-tuple-element.18), channel_id=3, replica_groups={{0,128},{8,136},{16,144},{24,152},{32,160},{40,168},{48,176},{56,184},{..., dimensions={0}, use_global_device_ids=true | all-gather | bytes 49152 | tf_op jit(solution)/shard_map/all_gather | solution.py:523
  34.6 0.1 join_groups.1
  34.7 9.4 %all_to_all.16 = f32[208,1,128]{2,1,0:T(1,128)S(1)} all-to-all(f32[208,1,128]{2,1,0:T(1,128)S(1)} %bitcast.19), channel_id=1, replica_groups={{80,48,112,16,88,56,120,24,72,40,104,8,64,32,96,0},{208,176,240,144,216..., dimensions={0} | all-to-all | bytes 212992 | tf_op jit(solution)/shard_map/all_to_all | solution.py:506
  44.1 1.3 %early_update.1 = (f32[3,64,2048]{2,1,0:T(8,128)}, f32[8,128]{1,0:T(8,128)S(1)}) custom-call(f32[208,128]{1,0:T(8,128)S(1)} %bitcast.16, f32[3,64,2048]{2,1,0:T(8,128)S(1)} %get-tuple-element.23.g_ref, f32[64,128]{1,0:T(8,128)S(1)} %get-tuple-element.24.p_ref, f32[64,128]{1,0:T(8,128)S(1)} %get-tuple-element.25.q_ref), custom_call_target="tpu_custom_call" | custom-call | tf_op jit(solution)/shard_map/early_update/pallas_call | solution.py:541
  45.4 12.2 %all_to_all.17 = f32[8,1,128]{2,1,0:T(1,128)S(1)} all-to-all(f32[8,1,128]{2,1,0:T(1,128)S(1)} %bitcast.24), channel_id=1, replica_groups={{5,4,7,6,3,2,1,0},{13,12,15,14,11,10,9,8},{21,20,23,22,19,18,17,16},{29..., dimensions={0} | all-to-all | bytes 8192 | tf_op jit(solution)/shard_map/all_to_all | solution.py:506
  57.6 0.7 %late_update.1 = (f32[3,64,2048]{2,1,0:T(8,128)}, f32[1,1]{1,0:T(1,128)}) custom-call(f32[3,64,2048]{2,1,0:T(8,128)} %get-tuple-element.26.begun_hbm, f32[8,128]{1,0:T(8,128)S(1)} %bitcast.23, f32[208,128]{1,0:T(8,128)S(1)} %bitcast.17, f32[3,64,2048]{2,1,0:T(8,128)S(1)} %get-tuple-element.23.g_ref, ...), custom_call_target="tpu_custom_call", output_to_operand_aliasing={{0}: (0, {})} | custom-call | tf_op jit(solution)/shard_map/late_update/pallas_call | solution.py:558

commit v7 on v6

--- a/solution.py
+++ b/solution.py
@@ -13,7 +13,8 @@
 
 GROUP = 16
 GROUPS = 4
-ORDER = tuple(4 * z + y for y in (2, 3, 1, 0) for z in (2, 1, 3, 0))
+ORDER_OUT = tuple(4 * z + y for y in (2, 3, 1, 0) for z in (2, 3, 0, 1))
+ORDER_BACK = tuple(4 * z + y for y in (2, 3, 1, 0) for z in (2, 3, 0, 1))
 YZ_ORDER = (5, 4, 7, 6, 3, 2, 1, 0)
 LANES = 128
 CELLS = 64
@@ -120,7 +121,7 @@
     count = recv_ref.shape[0] // GROUP
     stride = block_ref.shape[0] // GROUP
     comps = count // 8
-    for i, place in enumerate(ORDER):
+    for i, place in enumerate(ORDER_OUT):
         to = stride * place
         block_ref[to : to + count, :] = recv_ref[count * i : count * (i + 1), :]
     width = comps * LANES
@@ -410,7 +411,7 @@
             part_i = value[:, i * LANES : (i + 1) * LANES]
             block_ref[pl.ds(4 * i + r, GROUP, stride=stride), :] = part_i
     block_ref[pl.ds(4 * comps, GROUP, stride=stride), :] = jnp.broadcast_to(energy, (GROUP, LANES))
-    for i, place in enumerate(ORDER):
+    for i, place in enumerate(ORDER_BACK):
         send_ref[count * i : count * (i + 1), :] = block_ref[stride * place : stride * place + count, :]
 
 
@@ -421,9 +422,9 @@
     first, last = p_ref[...], q_ref[...]
     copies = []
     for c in range(comps):
-        for j in range(GROUP):
+        for j, place in enumerate(ORDER_OUT):
             at = slice(j * LANES, (j + 1) * LANES)
-            base = stride * j + 4 * c
+            base = stride * ORDER_BACK.index(place) + 4 * c
             u_t, w_t, u, w = [recv_ref[base + r : base + r + 1, :] for r in range(4)]
             value = g_ref[c, :, at] - first * u_t - last * w_t
             out_ref[c, 0:8, at] = jnp.where(row8 == 0, u, value[0:8])
@@ -437,8 +438,7 @@
 
 
 def early_device():
-    place = lax.axis_index("yz")
-    return (place % 2 == 1) | (place == 0)
+    return lax.axis_index("yz") % 2 == 1
 
 
 def early_kernel(recv_ref, g_ref, p_ref, q_ref, out_hbm, energy_ref, out_ref, sems):
@@ -471,7 +471,8 @@
     width = comps * LANES
     send_rows, back_rows = 8 * comps + 1, 4 * comps + 1
     yz_count = lax.axis_size("yz")
-    groups = [[GROUP * t + i for i in ORDER] for t in range(GROUPS)]
+    groups_out = [[GROUP * t + i for i in ORDER_OUT] for t in range(GROUPS)]
+    groups_back = [[GROUP * t + i for i in ORDER_BACK] for t in range(GROUPS)]
     shape = functools.partial(jax.ShapeDtypeStruct, dtype=F32)
 
     g, send, p_rows, q_rows = pl.pallas_call(
@@ -505,7 +506,7 @@
         rows = value.reshape(value.shape[0], 1, LANES)
         return lax.all_to_all(rows, axis, 0, 0, tiled=True, **kwargs).reshape(value.shape)
 
-    recv = spread(send, "gx", axis_index_groups=groups)
+    recv = spread(send, "gx", axis_index_groups=groups_out)
     msg, state, opened = pl.pallas_call(
         group_kernel,
         out_shape=[
@@ -537,7 +538,7 @@
         compiler_params=SMALL,
         name="join_groups",
     )(every, pair_state, pair_open, state, opened)
-    back = spread(send_back, "gx", axis_index_groups=groups)
+    back = spread(send_back, "gx", axis_index_groups=groups_back)
     begun, energy = pl.pallas_call(
         early_kernel,
         in_specs=[pl.BlockSpec(memory_space=pltpu.VMEM)] * 4,

time: 58.5 us -> 57.5 us (0.983)
  blocking collectives: 52.5 us -> 51.6 us
    all_to_all x3, blocking collectives: 35.2 us -> 34.2 us  [spread(): lax.all_to_all(rows, axis, 0, 0, tiled=True, **kwargs).reshape(value.shape)]
where the time goes in v7:
time: 57.5 us; the launch traced here: 57.3 us
  blocking collectives  51.6 us (90%)
  Pallas kernels  5.03 us (9%)
  between operations  0.67 us (1%)
    all_to_all x3, blocking collectives, spread(): lax.all_to_all(rows, axis, 0, 0, tiled=True, **kwargs).reshape(value.shape)  34.2 us
    all_gather x2, blocking collectives, joined(): return lax.all_gather(value, 'gx', axis_index_groups=members)  17.3 us
    pallas_call x1, Pallas kernels, on_device(): pl.pallas_call(local_kernel, in_specs=[pl.BlockSpec(memory_space=pltpu.HB...  2.55 us
    pallas_call x1, Pallas kernels, on_device(): pl.pallas_call(early_kernel, in_specs=[pl.BlockSpec(memory_space=pltpu.VM...  1.27 us

profile of v7, /device:TPU:1, one launch (start us, length us, event | category | flops | bytes accessed | tf_op | source)
XLA Modules:
  0.0 57.3 jit_solution(14931364392545556659)
XLA Ops:
  0.6 2.6 %local_solve.1 = (f32[3,64,2048]{2,1,0:T(8,128)S(1)}, f32[400,128]{1,0:T(8,128)S(1)}, f32[64,128]{1,0:T(8,128)S(1)}, f32[64,128]{1,0:T(8,128)S(1)}) custom-call(f32[3,64,2048]{2,1,0:T(8,128)} %v_hbm.1, f32[62,1,62]{2,1,0:T(1,128)} %bitcast.25), custom_call_target="tpu_custom_call" | custom-call | tf_op jit(solution)/shard_map/local_solve/pallas_call | solution.py:478
  3.2 13.6 %all_to_all.15 = f32[400,1,128]{2,1,0:T(1,128)S(1)} all-to-all(f32[400,1,128]{2,1,0:T(1,128)S(1)} %bitcast.20), channel_id=1, replica_groups={{80,112,16,48,88,120,24,56,72,104,8,40,64,96,0,32},{208,240,144,176,216..., dimensions={0} | all-to-all | bytes 409600 | tf_op jit(solution)/shard_map/all_to_all | solution.py:507
  16.8 0.3 group_solve.1
  17.1 10.2 %all-gather = f32[16,512]{1,0:T(8,128)S(1)} all-gather(f32[8,512]{1,0:T(8,128)S(1)} %get-tuple-element.17), channel_id=2, replica_groups={{384,0},{392,8},{400,16},{408,24},{416,32},{424,40},{432,48},{440,56},{..., dimensions={0}, use_global_device_ids=true | all-gather | bytes 49152 | tf_op jit(solution)/shard_map/all_gather | solution.py:524
  27.3 0.1 pair_groups.1
  27.4 7.2 %all-gather.1 = f32[16,512]{1,0:T(8,128)S(1)} all-gather(f32[8,512]{1,0:T(8,128)S(1)} %get-tuple-element.18), channel_id=3, replica_groups={{0,128},{8,136},{16,144},{24,152},{32,160},{40,168},{48,176},{56,184},{..., dimensions={0}, use_global_device_ids=true | all-gather | bytes 49152 | tf_op jit(solution)/shard_map/all_gather | solution.py:524
  34.5 0.1 join_groups.1
  34.7 9.6 %all_to_all.16 = f32[208,1,128]{2,1,0:T(1,128)S(1)} all-to-all(f32[208,1,128]{2,1,0:T(1,128)S(1)} %bitcast.19), channel_id=1, replica_groups={{80,112,16,48,88,120,24,56,72,104,8,40,64,96,0,32},{208,240,144,176,216..., dimensions={0} | all-to-all | bytes 212992 | tf_op jit(solution)/shard_map/all_to_all | solution.py:507
  44.3 1.3 %early_update.1 = (f32[3,64,2048]{2,1,0:T(8,128)}, f32[8,128]{1,0:T(8,128)S(1)}) custom-call(f32[208,128]{1,0:T(8,128)S(1)} %bitcast.16, f32[3,64,2048]{2,1,0:T(8,128)S(1)} %get-tuple-element.23.g_ref, f32[64,128]{1,0:T(8,128)S(1)} %get-tuple-element.24.p_ref, f32[64,128]{1,0:T(8,128)S(1)} %get-tuple-element.25.q_ref), custom_call_target="tpu_custom_call" | custom-call | tf_op jit(solution)/shard_map/early_update/pallas_call | solution.py:542
  45.6 11.0 %all_to_all.17 = f32[8,1,128]{2,1,0:T(1,128)S(1)} all-to-all(f32[8,1,128]{2,1,0:T(1,128)S(1)} %bitcast.24), channel_id=1, replica_groups={{5,4,7,6,3,2,1,0},{13,12,15,14,11,10,9,8},{21,20,23,22,19,18,17,16},{29..., dimensions={0} | all-to-all | bytes 8192 | tf_op jit(solution)/shard_map/all_to_all | solution.py:507
  56.6 0.7 %late_update.1 = (f32[3,64,2048]{2,1,0:T(8,128)}, f32[1,1]{1,0:T(1,128)}) custom-call(f32[3,64,2048]{2,1,0:T(8,128)} %get-tuple-element.26.begun_hbm, f32[8,128]{1,0:T(8,128)S(1)} %bitcast.23, f32[208,128]{1,0:T(8,128)S(1)} %bitcast.17, f32[3,64,2048]{2,1,0:T(8,128)S(1)} %get-tuple-element.23.g_ref, ...), custom_call_target="tpu_custom_call", output_to_operand_aliasing={{0}: (0, {})} | custom-call | tf_op jit(solution)/shard_map/late_update/pallas_call | solution.py:559

commit v8 on v7

--- a/solution.py
+++ b/solution.py
@@ -15,7 +15,7 @@
 GROUPS = 4
 ORDER_OUT = tuple(4 * z + y for y in (2, 3, 1, 0) for z in (2, 3, 0, 1))
 ORDER_BACK = tuple(4 * z + y for y in (2, 3, 1, 0) for z in (2, 3, 0, 1))
-YZ_ORDER = (5, 4, 7, 6, 3, 2, 1, 0)
+YZ_ORDER = (5, 4, 3, 2, 7, 6, 1, 0)
 LANES = 128
 CELLS = 64
 CHUNK = 512
@@ -430,9 +430,16 @@
             out_ref[c, 0:8, at] = jnp.where(row8 == 0, u, value[0:8])
             out_ref[c, 8 : CELLS - 8, at] = value[8 : CELLS - 8]
             out_ref[c, CELLS - 8 :, at] = jnp.where(row8 == 7, w, value[CELLS - 8 :])
-        copy = pltpu.make_async_copy(out_ref.at[c], out_hbm.at[c], sems.at[c])
-        copy.start()
-        copies.append(copy)
+            if c == comps - 1 and j == GROUP // 2 - 1:
+                half = (c, slice(None), pl.ds(0, lines // 2))
+                copies.append(pltpu.make_async_copy(out_ref.at[half], out_hbm.at[half], sems.at[c]))
+                copies[-1].start()
+        if c < comps - 1:
+            copies.append(pltpu.make_async_copy(out_ref.at[c], out_hbm.at[c], sems.at[c]))
+        else:
+            half = (c, slice(None), pl.ds(lines // 2, lines // 2))
+            copies.append(pltpu.make_async_copy(out_ref.at[half], out_hbm.at[half], sems.at[comps]))
+        copies[-1].start()
     for copy in copies:
         copy.wait()
 
@@ -456,7 +463,7 @@
 ):
     comps = g_ref.shape[0]
     mean_ref[0, 0] = jnp.sum(energy_ref[...]) * scale
-    mean_copy = pltpu.make_async_copy(mean_ref, mean_hbm, sems.at[comps])
+    mean_copy = pltpu.make_async_copy(mean_ref, mean_hbm, sems.at[comps + 1])
     mean_copy.start()
 
     @pl.when(jnp.logical_not(early_device()))
@@ -549,7 +556,7 @@
         out_shape=[shape((comps, cells, lines)), shape((yz_count, LANES))],
         scratch_shapes=[
             pltpu.VMEM((comps, cells, lines), F32),
-            pltpu.SemaphoreType.DMA((comps,)),
+            pltpu.SemaphoreType.DMA((comps + 1,)),
         ],
         compiler_params=LARGE,
         name="early_update",
@@ -566,7 +573,7 @@
         scratch_shapes=[
             pltpu.SMEM((1, 1), F32),
             pltpu.VMEM((comps, cells, lines), F32),
-            pltpu.SemaphoreType.DMA((comps + 1,)),
+            pltpu.SemaphoreType.DMA((comps + 2,)),
         ],
         compiler_params=LARGE,
         name="late_update",

time: 57.5 us -> 57.5 us (level)
  no operation moved by 1% of the time
where the time goes in v8:
time: 57.5 us; the launch traced here: 57.3 us
  blocking collectives  51.6 us (90%)
  Pallas kernels  5.05 us (9%)
  between operations  0.67 us (1%)
    all_to_all x3, blocking collectives, spread(): lax.all_to_all(rows, axis, 0, 0, tiled=True, **kwargs).reshape(value.shape)  34.2 us
    all_gather x2, blocking collectives, joined(): return lax.all_gather(value, 'gx', axis_index_groups=members)  17.3 us
    pallas_call x1, Pallas kernels, on_device(): pl.pallas_call(local_kernel, in_specs=[pl.BlockSpec(memory_space=pltpu.HB...  2.55 us
    pallas_call x1, Pallas kernels, on_device(): pl.pallas_call(early_kernel, in_specs=[pl.BlockSpec(memory_space=pltpu.VM...  1.27 us

profile of v8, /device:TPU:1, one launch (start us, length us, event | category | flops | bytes accessed | tf_op | source)
XLA Modules:
  0.0 57.3 jit_solution(17536777500018581434)
XLA Ops:
  0.6 2.6 %local_solve.1 = (f32[3,64,2048]{2,1,0:T(8,128)S(1)}, f32[400,128]{1,0:T(8,128)S(1)}, f32[64,128]{1,0:T(8,128)S(1)}, f32[64,128]{1,0:T(8,128)S(1)}) custom-call(f32[3,64,2048]{2,1,0:T(8,128)} %v_hbm.1, f32[62,1,62]{2,1,0:T(1,128)} %bitcast.25), custom_call_target="tpu_custom_call" | custom-call | tf_op jit(solution)/shard_map/local_solve/pallas_call | solution.py:485
  3.2 13.6 %all_to_all.15 = f32[400,1,128]{2,1,0:T(1,128)S(1)} all-to-all(f32[400,1,128]{2,1,0:T(1,128)S(1)} %bitcast.20), channel_id=1, replica_groups={{80,112,16,48,88,120,24,56,72,104,8,40,64,96,0,32},{208,240,144,176,216..., dimensions={0} | all-to-all | bytes 409600 | tf_op jit(solution)/shard_map/all_to_all | solution.py:514
  16.8 0.3 group_solve.1
  17.1 10.2 %all-gather = f32[16,512]{1,0:T(8,128)S(1)} all-gather(f32[8,512]{1,0:T(8,128)S(1)} %get-tuple-element.17), channel_id=2, replica_groups={{384,0},{392,8},{400,16},{408,24},{416,32},{424,40},{432,48},{440,56},{..., dimensions={0}, use_global_device_ids=true | all-gather | bytes 49152 | tf_op jit(solution)/shard_map/all_gather | solution.py:531
  27.3 0.1 pair_groups.1
  27.4 7.2 %all-gather.1 = f32[16,512]{1,0:T(8,128)S(1)} all-gather(f32[8,512]{1,0:T(8,128)S(1)} %get-tuple-element.18), channel_id=3, replica_groups={{0,128},{8,136},{16,144},{24,152},{32,160},{40,168},{48,176},{56,184},{..., dimensions={0}, use_global_device_ids=true | all-gather | bytes 49152 | tf_op jit(solution)/shard_map/all_gather | solution.py:531
  34.5 0.1 join_groups.1
  34.7 9.6 %all_to_all.16 = f32[208,1,128]{2,1,0:T(1,128)S(1)} all-to-all(f32[208,1,128]{2,1,0:T(1,128)S(1)} %bitcast.19), channel_id=1, replica_groups={{80,112,16,48,88,120,24,56,72,104,8,40,64,96,0,32},{208,240,144,176,216..., dimensions={0} | all-to-all | bytes 212992 | tf_op jit(solution)/shard_map/all_to_all | solution.py:514
  44.3 1.3 %early_update.1 = (f32[3,64,2048]{2,1,0:T(8,128)}, f32[8,128]{1,0:T(8,128)S(1)}) custom-call(f32[208,128]{1,0:T(8,128)S(1)} %bitcast.16, f32[3,64,2048]{2,1,0:T(8,128)S(1)} %get-tuple-element.23.g_ref, f32[64,128]{1,0:T(8,128)S(1)} %get-tuple-element.24.p_ref, f32[64,128]{1,0:T(8,128)S(1)} %get-tuple-element.25.q_ref), custom_call_target="tpu_custom_call" | custom-call | tf_op jit(solution)/shard_map/early_update/pallas_call | solution.py:549
  45.6 11.0 %all_to_all.17 = f32[8,1,128]{2,1,0:T(1,128)S(1)} all-to-all(f32[8,1,128]{2,1,0:T(1,128)S(1)} %bitcast.24), channel_id=1, replica_groups={{5,4,3,2,7,6,1,0},{13,12,11,10,15,14,9,8},{21,20,19,18,23,22,17,16},{29..., dimensions={0} | all-to-all | bytes 8192 | tf_op jit(solution)/shard_map/all_to_all | solution.py:514
  56.6 0.7 %late_update.1 = (f32[3,64,2048]{2,1,0:T(8,128)}, f32[1,1]{1,0:T(1,128)}) custom-call(f32[3,64,2048]{2,1,0:T(8,128)} %get-tuple-element.26.begun_hbm, f32[8,128]{1,0:T(8,128)S(1)} %bitcast.23, f32[208,128]{1,0:T(8,128)S(1)} %bitcast.17, f32[3,64,2048]{2,1,0:T(8,128)S(1)} %get-tuple-element.23.g_ref, ...), custom_call_target="tpu_custom_call", output_to_operand_aliasing={{0}: (0, {})} | custom-call | tf_op jit(solution)/shard_map/late_update/pallas_call | solution.py:566

commit v9 on v8

--- a/solution.py
+++ b/solution.py
@@ -430,14 +430,14 @@
             out_ref[c, 0:8, at] = jnp.where(row8 == 0, u, value[0:8])
             out_ref[c, 8 : CELLS - 8, at] = value[8 : CELLS - 8]
             out_ref[c, CELLS - 8 :, at] = jnp.where(row8 == 7, w, value[CELLS - 8 :])
-            if c == comps - 1 and j == GROUP // 2 - 1:
-                half = (c, slice(None), pl.ds(0, lines // 2))
+            if c == comps - 1 and j == 3 * GROUP // 4 - 1:
+                half = (c, slice(None), pl.ds(0, 3 * lines // 4))
                 copies.append(pltpu.make_async_copy(out_ref.at[half], out_hbm.at[half], sems.at[c]))
                 copies[-1].start()
         if c < comps - 1:
             copies.append(pltpu.make_async_copy(out_ref.at[c], out_hbm.at[c], sems.at[c]))
         else:
-            half = (c, slice(None), pl.ds(lines // 2, lines // 2))
+            half = (c, slice(None), pl.ds(3 * lines // 4, lines // 4))
             copies.append(pltpu.make_async_copy(out_ref.at[half], out_hbm.at[half], sems.at[comps]))
         copies[-1].start()
     for copy in copies:

time: 57.5 us -> 57.5 us (level)
  no operation moved by 1% of the time
where the time goes in v9:
time: 57.5 us; the launch traced here: 57.3 us
  blocking collectives  51.6 us (90%)
  Pallas kernels  5.04 us (9%)
  between operations  0.67 us (1%)
    all_to_all x3, blocking collectives, spread(): lax.all_to_all(rows, axis, 0, 0, tiled=True, **kwargs).reshape(value.shape)  34.2 us
    all_gather x2, blocking collectives, joined(): return lax.all_gather(value, 'gx', axis_index_groups=members)  17.3 us
    pallas_call x1, Pallas kernels, on_device(): pl.pallas_call(local_kernel, in_specs=[pl.BlockSpec(memory_space=pltpu.HB...  2.55 us
    pallas_call x1, Pallas kernels, on_device(): pl.pallas_call(early_kernel, in_specs=[pl.BlockSpec(memory_space=pltpu.VM...  1.27 us

profile of v9, /device:TPU:1, one launch (start us, length us, event | category | flops | bytes accessed | tf_op | source)
XLA Modules:
  0.0 57.3 jit_solution(9859477111273832827)
XLA Ops:
  0.6 2.6 %local_solve.1 = (f32[3,64,2048]{2,1,0:T(8,128)S(1)}, f32[400,128]{1,0:T(8,128)S(1)}, f32[64,128]{1,0:T(8,128)S(1)}, f32[64,128]{1,0:T(8,128)S(1)}) custom-call(f32[3,64,2048]{2,1,0:T(8,128)} %v_hbm.1, f32[62,1,62]{2,1,0:T(1,128)} %bitcast.25), custom_call_target="tpu_custom_call" | custom-call | tf_op jit(solution)/shard_map/local_solve/pallas_call | solution.py:485
  3.2 13.6 %all_to_all.15 = f32[400,1,128]{2,1,0:T(1,128)S(1)} all-to-all(f32[400,1,128]{2,1,0:T(1,128)S(1)} %bitcast.20), channel_id=1, replica_groups={{80,112,16,48,88,120,24,56,72,104,8,40,64,96,0,32},{208,240,144,176,216..., dimensions={0} | all-to-all | bytes 409600 | tf_op jit(solution)/shard_map/all_to_all | solution.py:514
  16.8 0.3 group_solve.1
  17.1 10.2 %all-gather = f32[16,512]{1,0:T(8,128)S(1)} all-gather(f32[8,512]{1,0:T(8,128)S(1)} %get-tuple-element.17), channel_id=2, replica_groups={{384,0},{392,8},{400,16},{408,24},{416,32},{424,40},{432,48},{440,56},{..., dimensions={0}, use_global_device_ids=true | all-gather | bytes 49152 | tf_op jit(solution)/shard_map/all_gather | solution.py:531
  27.3 0.1 pair_groups.1
  27.4 7.2 %all-gather.1 = f32[16,512]{1,0:T(8,128)S(1)} all-gather(f32[8,512]{1,0:T(8,128)S(1)} %get-tuple-element.18), channel_id=3, replica_groups={{0,128},{8,136},{16,144},{24,152},{32,160},{40,168},{48,176},{56,184},{..., dimensions={0}, use_global_device_ids=true | all-gather | bytes 49152 | tf_op jit(solution)/shard_map/all_gather | solution.py:531
  34.5 0.1 join_groups.1
  34.7 9.6 %all_to_all.16 = f32[208,1,128]{2,1,0:T(1,128)S(1)} all-to-all(f32[208,1,128]{2,1,0:T(1,128)S(1)} %bitcast.19), channel_id=1, replica_groups={{80,112,16,48,88,120,24,56,72,104,8,40,64,96,0,32},{208,240,144,176,216..., dimensions={0} | all-to-all | bytes 212992 | tf_op jit(solution)/shard_map/all_to_all | solution.py:514
  44.3 1.3 %early_update.1 = (f32[3,64,2048]{2,1,0:T(8,128)}, f32[8,128]{1,0:T(8,128)S(1)}) custom-call(f32[208,128]{1,0:T(8,128)S(1)} %bitcast.16, f32[3,64,2048]{2,1,0:T(8,128)S(1)} %get-tuple-element.23.g_ref, f32[64,128]{1,0:T(8,128)S(1)} %get-tuple-element.24.p_ref, f32[64,128]{1,0:T(8,128)S(1)} %get-tuple-element.25.q_ref), custom_call_target="tpu_custom_call" | custom-call | tf_op jit(solution)/shard_map/early_update/pallas_call | solution.py:549
  45.6 11.0 %all_to_all.17 = f32[8,1,128]{2,1,0:T(1,128)S(1)} all-to-all(f32[8,1,128]{2,1,0:T(1,128)S(1)} %bitcast.24), channel_id=1, replica_groups={{5,4,3,2,7,6,1,0},{13,12,11,10,15,14,9,8},{21,20,19,18,23,22,17,16},{29..., dimensions={0} | all-to-all | bytes 8192 | tf_op jit(solution)/shard_map/all_to_all | solution.py:514
  56.6 0.7 %late_update.1 = (f32[3,64,2048]{2,1,0:T(8,128)}, f32[1,1]{1,0:T(1,128)}) custom-call(f32[3,64,2048]{2,1,0:T(8,128)} %get-tuple-element.26.begun_hbm, f32[8,128]{1,0:T(8,128)S(1)} %bitcast.23, f32[208,128]{1,0:T(8,128)S(1)} %bitcast.17, f32[3,64,2048]{2,1,0:T(8,128)S(1)} %get-tuple-element.23.g_ref, ...), custom_call_target="tpu_custom_call", output_to_operand_aliasing={{0}: (0, {})} | custom-call | tf_op jit(solution)/shard_map/late_update/pallas_call | solution.py:566
